TPU v7x, 256 devices: a whole 4x4x8 slice. The times are simulated.
256 devices in a mesh: seq: 16 (over y, x), head: 16 (over z, core).
Axes of the slice: x: 4, y: 4, z: 8, core: 2. Of those that a mesh axis runs over, the one named last changes fastest.
Arguments:
- x_in: bfloat16 [2, 4096, 8192], P(None, ('seq', 'head')), may hold values from -6 to 6
- b_in: bfloat16 [2, 4096, 2048], P(None, ('seq', 'head')), may hold values from -6 to 6
- c_in: bfloat16 [2, 4096, 2048], P(None, ('seq', 'head')), may hold values from -0.375 to 0.375
- dt_in: bfloat16 [2, 4096, 128], P(None, ('seq', 'head')), may hold values from -7 to 5
- a_log: float32 [128], P('head'), may hold values from -6 to -2
- skip_gain: float32 [128], P('head'), may hold values from 0.5 to 1.5
- grad_y: bfloat16 [2, 4096, 8192], P(None, 'seq', 'head'), may hold values from -4 to 4
Outputs:
- y_out: bfloat16 [2, 4096, 8192], P(None, 'seq', 'head')
- grad_x: bfloat16 [2, 4096, 8192], P(None, ('seq', 'head'))
- grad_b: bfloat16 [2, 4096, 2048], P(None, ('seq', 'head'))
- grad_c: bfloat16 [2, 4096, 2048], P(None, ('seq', 'head'))
- grad_dt: bfloat16 [2, 4096, 128], P(None, ('seq', 'head'))
All inputs are finite; a program needn't handle non-finite values.
Results may differ from a plain program's by a relative error of at most 0.003.
Values may be sent and summed in bfloat16 or wider, within the bound.
A program may use at most 128 MiB of HBM per device.

v0:
```python
from functools import partial

import jax
import jax.numpy as jnp
from jax import lax
from jax.sharding import PartitionSpec as P

HEAD_DIM = 64
STATE = 256
STRETCH = 256


highest = lax.Precision.HIGHEST


def prefix(part, axis, combine, identity, reverse):
    count = lax.axis_size(axis)
    place = lax.axis_index(axis)
    ahead = count - 1 - place if reverse else place
    gathered = jax.tree.map(lambda a: lax.all_gather(a, axis), part)
    state = jax.tree.map(lambda a, e: jnp.zeros_like(a) + jnp.asarray(e, a.dtype), part, identity)

    def one(hop, state):
        source = count - 1 - hop if reverse else hop
        return combine(
            state, jax.tree.map(lambda a: lax.dynamic_index_in_dim(a, source, 0, False), gathered)
        )

    return lax.fori_loop(0, ahead, one, state)


def carry_state(carried, x_vals, b_vals, dt_vals, cum_vals):
    final_cum = cum_vals[-1]
    weight = jnp.exp(final_cum[None] - cum_vals) * dt_vals
    update = jnp.einsum("tjep,tjn->jepn", x_vals * weight[..., None], b_vals, precision=highest)
    return jnp.exp(final_cum)[..., None, None] * carried + update


def stretched_step_update(carried, x_vals, b_vals, c_vals, dt_vals, cum_vals, skip_rows):
    scores = jnp.einsum("tjn,ujn->jtu", c_vals, b_vals, precision=highest)
    token_positions = jnp.arange(x_vals.shape[0])
    causal = token_positions[:, None] >= token_positions[None, :]
    cum_rows = jnp.moveaxis(cum_vals, 0, 2)
    log_gap = cum_rows[..., :, None] - cum_rows[..., None, :]
    decays = jnp.where(causal, jnp.exp(jnp.where(causal, log_gap, 0.0)), 0.0)
    mixing = scores[:, None] * decays * jnp.moveaxis(dt_vals, 0, 2)[:, :, None, :]
    within = jnp.einsum("jetu,ujep->tjep", mixing, x_vals, precision=highest)
    carried_part = (
        jnp.einsum("tjn,jepn->tjep", c_vals, carried, precision=highest)
        * jnp.exp(cum_vals)[..., None]
    )
    result = within + carried_part + skip_rows[:, :, None] * x_vals
    return (carry_state(carried, x_vals, b_vals, dt_vals, cum_vals), result)


def scan_step(carried, inputs, decay_rate, skip_rows):
    x_vals, b_vals, c_vals, dt_raw = inputs
    dt_vals = jax.nn.softplus(dt_raw.astype(jnp.float32))
    cum_vals = jnp.cumsum(dt_vals * decay_rate, axis=1)

    def single(state_one, x_one, b_one, c_one, dt_one, cum_one):
        return stretched_step_update(state_one, x_one, b_one, c_one, dt_one, cum_one, skip_rows)

    return jax.vmap(single)(
        carried,
        x_vals.astype(jnp.float32),
        b_vals.astype(jnp.float32),
        c_vals.astype(jnp.float32),
        dt_vals,
        cum_vals,
    )


def link_states(earlier, later):
    return (earlier[0] + later[0], jnp.exp(later[0])[..., None, None] * earlier[1] + later[1])


def on_device(x_in, b_in, c_in, dt_in, a_log, skip_gain, grad_y):
    seq_count = x_in.shape[0]
    row_count = x_in.shape[1]
    heads_dev = a_log.shape[0]
    parts = lax.axis_size("head")
    groups = b_in.shape[2] // STATE
    repeat = parts // groups
    decay_rate = -jnp.exp(a_log).reshape(1, heads_dev)
    skip_rows = skip_gain.reshape(1, heads_dev)

    def by_part(array, width):
        return array.reshape(seq_count, row_count, parts, width)

    def spread_groups(array):
        return jnp.repeat(array.reshape(seq_count, row_count, groups, STATE), repeat, axis=2)

    x_part, b_part, c_part, dt_part = (
        lax.all_to_all(
            by_part(x_in, heads_dev * HEAD_DIM), "head", split_axis=2, concat_axis=1, tiled=True
        ),
        lax.all_to_all(spread_groups(b_in), "head", split_axis=2, concat_axis=1, tiled=True),
        lax.all_to_all(spread_groups(c_in), "head", split_axis=2, concat_axis=1, tiled=True),
        lax.all_to_all(by_part(dt_in, heads_dev), "head", split_axis=2, concat_axis=1, tiled=True),
    )
    rows_all = x_part.shape[1]
    stretches = rows_all // STRETCH

    def by_stretch(array):
        return jnp.moveaxis(array.reshape((seq_count, stretches, STRETCH) + array.shape[2:]), 1, 0)

    def heads_view(x_vals):
        return x_vals.reshape(seq_count, rows_all, 1, heads_dev, HEAD_DIM)

    def local_scan(x_vals, b_vals, c_vals, dt_vals, start):
        stepper = jax.checkpoint(partial(scan_step, decay_rate=decay_rate, skip_rows=skip_rows))
        final_state, outputs = lax.scan(
            stepper,
            start,
            (
                by_stretch(heads_view(x_vals)),
                by_stretch(b_vals),
                by_stretch(c_vals),
                by_stretch(dt_vals),
            ),
        )
        return (
            jnp.moveaxis(outputs, 0, 1).reshape(seq_count, rows_all, heads_dev * HEAD_DIM),
            final_state,
        )

    def advance(carry_pair, inputs):
        carried, totals = carry_pair
        x_vals, b_vals, dt_raw = inputs
        dt_vals = jax.nn.softplus(dt_raw.astype(jnp.float32))
        cum_vals = jnp.cumsum(dt_vals * decay_rate, axis=1)
        updated = jax.vmap(carry_state)(
            carried, x_vals.astype(jnp.float32), b_vals.astype(jnp.float32), dt_vals, cum_vals
        )
        return ((updated, totals + cum_vals[:, -1]), None)

    zero_state = jnp.zeros((seq_count, 1, heads_dev, HEAD_DIM, STATE), jnp.float32)
    zero_totals = jnp.zeros((seq_count, 1, heads_dev), jnp.float32)
    (closing_local_state, totals), unused = lax.scan(
        advance,
        (zero_state, zero_totals),
        (by_stretch(heads_view(x_part)), by_stretch(b_part), by_stretch(dt_part)),
    )
    h_in = prefix(
        (totals, closing_local_state), "seq", link_states, (zero_totals, zero_state), False
    )[1]
    (mixed_out, h_out), pullback = jax.vjp(local_scan, x_part, b_part, c_part, dt_part, h_in)
    upstream = grad_y.astype(jnp.float32)
    from_outputs = pullback((upstream, jnp.zeros_like(h_out)))[4]
    downstream = prefix(
        (totals, from_outputs), "seq", link_states, (zero_totals, zero_state), True
    )[1]
    grad_x_part, grad_b_part, grad_c_part, grad_dt_part, unused_grad = pullback(
        (upstream, downstream)
    )
    grad_x_back, grad_b_back, grad_c_back, grad_dt_back = (
        lax.all_to_all(grad_x_part, "head", split_axis=1, concat_axis=2, tiled=True),
        lax.all_to_all(grad_b_part, "head", split_axis=1, concat_axis=2, tiled=True),
        lax.all_to_all(grad_c_part, "head", split_axis=1, concat_axis=2, tiled=True),
        lax.all_to_all(grad_dt_part, "head", split_axis=1, concat_axis=2, tiled=True),
    )

    def group_sum(slices):
        summed = (
            slices.astype(jnp.float32)
            .reshape(seq_count, row_count, groups, repeat, STATE)
            .sum(axis=3)
        )
        return summed.astype(jnp.bfloat16).reshape(seq_count, row_count, groups * STATE)

    grad_x = grad_x_back.reshape(seq_count, row_count, parts * heads_dev * HEAD_DIM)
    grad_dt = grad_dt_back.reshape(seq_count, row_count, parts * heads_dev)
    return (
        mixed_out.astype(jnp.bfloat16),
        grad_x,
        group_sum(grad_b_back),
        group_sum(grad_c_back),
        grad_dt,
    )


def solution(mesh):
    return jax.shard_map(
        on_device,
        mesh=mesh,
        in_specs=(
            P(None, ("seq", "head"), None),
            P(None, ("seq", "head"), None),
            P(None, ("seq", "head"), None),
            P(None, ("seq", "head"), None),
            P("head"),
            P("head"),
            P(None, "seq", "head"),
        ),
        out_specs=(
            P(None, "seq", "head"),
            P(None, ("seq", "head"), None),
            P(None, ("seq", "head"), None),
            P(None, ("seq", "head"), None),
            P(None, ("seq", "head"), None),
        ),
        check_vma=False,
    )
```

profile of v0, /device:TPU:31, one launch (start us, length us, event | category | flops | bytes accessed | tf_op | source)
XLA Modules:
  0.0 450.4 jit_solution(16844222990921493420)
XLA Ops:
  8.7 9.2 %all-to-all-start.2 = ((bf16[16,2,128]{2,1,0:T(2,128)(2,1)}), bf16[16,2,128]{2,1,0:T(2,128)(2,1)S(1)}, u32[]{:S(2)}, u32[]{:S(2)}) async-start(bf16[16,2,128]{2,1,0:T(2,128)(2,1)} %reshape.900), calls=%async_computation.2 | async-start | bytes 16384 | tf_op jit(solution)/shard_map/all_to_all | solution.py:100
  18.8 6.0 %all-to-all-done.2 = bf16[16,2,128]{2,1,0:T(2,128)(2,1)S(1)} async-done(((bf16[16,2,128]{2,1,0:T(2,128)(2,1)}), bf16[16,2,128]{2,1,0:T(2,128)(2,1)S(1)}, u32[]{:S(2)}, u32[]{:S(2)}) %all-to-all-start.2) | async-done | bytes 8224 | tf_op jit(solution)/shard_map/all_to_all | solution.py:100
  25.5 4.0 all-to-all-start
  31.8 9.6 %all-to-all-done = bf16[2,16,16,256]{3,1,0,2:T(8,128)(2,1)S(1)} async-done(((bf16[2,16,16,256]{3,1,0,2:T(8,128)(2,1)}), bf16[2,16,16,256]{3,1,0,2:T(8,128)(2,1)S(1)}, u32[]{:S(2)}, u32[]{:S(2)}) %all-to-all-start) | async-done | bytes 262176 | tf_op jit(solution)/shard_map/all_to_all | solution.py:99
  46.4 3.4 all-to-all-start.1
  52.9 8.0 %all-to-all-done.1 = bf16[2,16,16,256]{3,1,0,2:T(8,128)(2,1)S(1)} async-done(((bf16[2,16,16,256]{3,1,0,2:T(8,128)(2,1)}), bf16[2,16,16,256]{3,1,0,2:T(8,128)(2,1)S(1)}, u32[]{:S(2)}, u32[]{:S(2)}) %all-to-all-start.1) | async-done | bytes 262176 | tf_op jit(solution)/shard_map/all_to_all | solution.py:98
  60.9 3.5 all-to-all-start.3
  67.0 14.2 %all-to-all-done.3 = bf16[2,16,16,512]{3,1,0,2:T(8,128)(2,1)S(1)} async-done(((bf16[2,16,16,512]{3,1,0,2:T(8,128)(2,1)}), bf16[2,16,16,512]{3,1,0,2:T(8,128)(2,1)S(1)}, u32[]{:S(2)}, u32[]{:S(2)}) %all-to-all-start.3) | async-done | bytes 524320 | tf_op jit(solution)/shard_map/all_to_all | solution.py:95
  86.2 18.0 %all-gather = f32[32,1,1,8]{3,2,1,0:T(1,128)S(1)} all-gather(f32[2,1,1,8]{3,2,1,0:T(1,128)S(1)} %bitcast.462), channel_id=2, replica_groups=mesh['seq'=16,'head'=16] {'seq'}, dimensions={0}, use_global_device_ids=true | all-gather | bytes 1088 | tf_op jit(solution)/shard_map/all_gather | solution.py:20
  106.6 50.1 %all-gather.8.cloned.1.call-done = f32[32,1,8,64,256]{4,3,2,1,0:T(8,128)} async-done(((f32[2,1,8,64,256]{4,3,2,1,0:T(8,128)}), f32[32,1,8,64,256]{4,3,2,1,0:T(8,128)}) %all-gather.8.cloned.1.call-update) | async-done | bytes 16777232 | tf_op jit(solution)/shard_map/all_gather | solution.py:20
  156.7 118.5 %all-gather.6.cloned.1.call-done = f32[32,8,64,256]{3,2,1,0:T(8,128)} async-done(((f32[2,8,64,256]{3,2,1,0:T(8,128)}), f32[32,8,64,256]{3,2,1,0:T(8,128)}) %all-gather.6.cloned.1.call-update) | async-done | bytes 16777232 | tf_op jit(solution)/shard_map/all_gather | solution.py:20
  275.2 23.0 %while.18 = (s32[]{:T(128)}, f32[2,1,8,64,256]{4,3,2,1,0:T(8,128)S(1)}, s32[]{:T(128)}, f32[16,2,1,8]{3,1,2,0:T(2,128)S(1)}, f32[16,2,1,8,64,256]{5,4,3,1,2,0:T(8,128)}, /*index=5*/s32[]{:T(128)}, s32[]{:T(128)}, s32[]{:T(128)}) while((s32[]{:T(128)}, f32[2,1,8,64,256]{4,3,2,1,0:T(8,128)S(1)}, s32[]{:T(128)}, f32[16,2,1,8]{3,1,2,0:T(2,128)S(1)}, ...), condition=%wide.region_3.4_spmd, body=%wide.region_2.3_spmd.sunk | while | flops 524293 | bytes 3146055 | solution.py:29
  317.0 3.4 fusion.57
  336.8 7.2 %fusion.13 = (f32[2,8,256]{2,1,0:T(8,128)}, f32[2,8,256]{2,1,0:T(8,128)}, f32[2,8,256]{2,1,0:T(8,128)}, f32[2,256,256]{2,1,0:T(8,128)}) fusion(f32[2,8,256]{2,1,0:T(8,128)} %copy.293, f32[2,8,256]{2,1,0:T(8,128)} %bitcast_add_fusion.7, f32[2,256,256]{2,1,0:T(8,128)} %fusion.99, pred[256,256]{1,0:T(8,128)(4,1)} %iota_compare_fusion, ...), kind=kOutput, calls=%fused_computation.20 | convolution fusion | flops 820891648 | bytes 2768896 | tf_op jit(solution)/shard_map/transpose(jvp())/while/body/eval_jaxpr/checkpoint/vmap(jetu,ujep->tjep)/dot_general | solution.py:47
  352.5 6.2 %reduce-window.54 = f32[2,8,1,2,128]{4,1,2,3,0:T(8,128)} reduce-window(f32[2,8,1,2,128]{4,1,2,3,0:T(8,128)} %copy.313, f32[]{:T(128)} %constant.147.clone.1), window={size=1x1x1x1x128 pad=0_0x0_0x0_0x0_0x0_127}, to_apply=%region_20.21 | reduce-window | flops 520192 | bytes 32772 | tf_op jit(solution)/shard_map/reduce-window.6
  373.4 7.7 %all-to-all-start.7 = ((bf16[16,2,128]{2,1,0:T(2,128)(2,1)}), bf16[16,2,128]{2,1,0:T(2,128)(2,1)S(1)}, u32[]{:S(2)}, u32[]{:S(2)}) async-start(bf16[16,2,128]{2,1,0:T(2,128)(2,1)} %reshape.902), calls=%async_computation.7 | async-start | bytes 16384 | tf_op jit(solution)/shard_map/all_to_all | solution.py:161
  381.1 3.8 fusion.53
  388.0 6.0 %all-to-all-start.5 = ((bf16[2,256,1,256]{3,0,2,1:T(2,128)(2,1)}), bf16[2,256,1,256]{3,0,2,1:T(2,128)(2,1)S(1)}, u32[]{:S(2)}, u32[]{:S(2)}) async-start(bf16[2,256,1,256]{3,0,2,1:T(2,128)(2,1)} %copy.301), calls=%async_computation.5 | async-start | bytes 524288 | tf_op jit(solution)/shard_map/all_to_all | solution.py:159
  399.3 6.4 %all-to-all-done.5 = bf16[2,256,1,256]{3,0,2,1:T(2,128)(2,1)S(1)} async-done(((bf16[2,256,1,256]{3,0,2,1:T(2,128)(2,1)}), bf16[2,256,1,256]{3,0,2,1:T(2,128)(2,1)S(1)}, u32[]{:S(2)}, u32[]{:S(2)}) %all-to-all-start.5) | async-done | bytes 262176 | tf_op jit(solution)/shard_map/all_to_all | solution.py:159
  405.7 3.4 all-to-all-start.6
  409.4 5.9 %fusion.47 = bf16[2,256,1,8,64]{1,4,3,0,2:T(8,128)(2,1)} fusion(f32[2,8,256]{2,1,0:T(8,128)S(1)} %copy-done.20, f32[2,8,256]{2,1,0:T(8,128)} %bitcast_add_fusion.7, f32[2,256,256]{2,1,0:T(8,128)} %fusion.99, pred[256,256]{1,0:T(8,128)(4,1)S(1)} %copy-done.16, f32[2,256,1,8,64]{1,4,3,0,2:T(8,128)S(1)} %bitcast.409, ...), kind=kOutput, calls=%fused_computation.53 | convolution fusion | flops 811859968 | bytes 3260448 | tf_op jit(solution)/shard_map/transpose(jvp())/while/body/eval_jaxpr/checkpoint/vmap(jetu,ujep->tjep)/dot_general | solution.py:47
  421.0 3.9 all-to-all-start.4
  428.5 5.1 %fusion.28 = f32[2,256,1,8,64]{1,4,3,0,2:T(8,128)S(1)} fusion(f32[2,8,256]{2,1,0:T(8,128)S(1)} %copy.266, f32[2,8,256]{2,1,0:T(8,128)S(1)} %bitcast_add_fusion.9, f32[2,256,256]{2,1,0:T(8,128)} %fusion.113, pred[256,256]{1,0:T(8,128)(4,1)S(1)} %copy-done.16, bf16[2,256,8,64]{3,2,1,0:T(8,128)(2,1)} %copy-done.5), kind=kOutput, calls=%fused_computation.36 | convolution fusion | flops 810549248 | bytes 2195456 | tf_op jit(solution)/shard_map/jvp()/while/body/eval_jaxpr/vmap(jetu,ujep->tjep)/dot_general | solution.py:47
  438.4 3.8 all-to-all-done.4
  (196 shorter events, 127.9 us)
Async XLA Ops:
  8.7 16.1 %all-to-all-start.2 = ((bf16[16,2,128]{2,1,0:T(2,128)(2,1)}), bf16[16,2,128]{2,1,0:T(2,128)(2,1)S(1)}, u32[]{:S(2)}, u32[]{:S(2)}) async-start(bf16[16,2,128]{2,1,0:T(2,128)(2,1)} %reshape.900), calls=%async_computation.2 | async-start | bytes 16384 | tf_op jit(solution)/shard_map/all_to_all | solution.py:100
  25.5 15.8 %all-to-all-start = ((bf16[2,16,16,256]{3,1,0,2:T(8,128)(2,1)}), bf16[2,16,16,256]{3,1,0,2:T(8,128)(2,1)S(1)}, u32[]{:S(2)}, u32[]{:S(2)}) async-start(bf16[2,16,16,256]{3,1,0,2:T(8,128)(2,1)} %bitcast.4), calls=%async_computation | async-start | bytes 524288 | tf_op jit(solution)/shard_map/all_to_all | solution.py:99
  29.5 16.2 %copy-start.15 = (bf16[2,16,2048]{2,1,0:T(8,128)(2,1)S(1)}, bf16[2,16,2048]{2,1,0:T(8,128)(2,1)}, u32[]{:S(2)}) copy-start(bf16[2,16,2048]{2,1,0:T(8,128)(2,1)} %param.12) | copy-start | bytes 393220
  29.5 127.2 %all-gather.8.cloned.1.call-start = ((), (), s32[]{:S(2)}) async-start(), calls=%async_computation.9 | async-start | bytes 17825792 | tf_op jit(solution)/shard_map/all_gather | solution.py:20
  31.5 14.9 %copy-start.21 = (f32[1,8]{1,0:T(1,128)}, f32[1,8]{1,0:T(1,128)S(1)}, u32[]{:S(2)}) copy-start(f32[1,8]{1,0:T(1,128)S(1)} %get-tuple-element.338) | copy-start | bytes 100
  31.6 18.3 %copy-start.13 = (bf16[2,16,8192]{2,1,0:T(8,128)(2,1)S(1)}, bf16[2,16,8192]{2,1,0:T(8,128)(2,1)}, u32[]{:S(2)}) copy-start(bf16[2,16,8192]{2,1,0:T(8,128)(2,1)} %param.11) | copy-start | bytes 1572868
  31.8 19.0 %copy-start.14 = (bf16[2,256,1,8]{1,3,0,2:T(8,128)(2,1)}, bf16[2,256,1,8]{1,3,0,2:T(8,128)(2,1)S(1)}, u32[]{:S(2)}) copy-start(bf16[2,256,1,8]{1,3,0,2:T(8,128)(2,1)S(1)} %squeeze.82) | copy-start | bytes 24580
  46.4 14.5 %all-to-all-start.1 = ((bf16[2,16,16,256]{3,1,0,2:T(8,128)(2,1)}), bf16[2,16,16,256]{3,1,0,2:T(8,128)(2,1)S(1)}, u32[]{:S(2)}, u32[]{:S(2)}) async-start(bf16[2,16,16,256]{3,1,0,2:T(8,128)(2,1)} %bitcast.8), calls=%async_computation.1 | async-start | bytes 524288 | tf_op jit(solution)/shard_map/all_to_all | solution.py:98
  60.9 20.4 %all-to-all-start.3 = ((bf16[2,16,16,512]{3,1,0,2:T(8,128)(2,1)}), bf16[2,16,16,512]{3,1,0,2:T(8,128)(2,1)S(1)}, u32[]{:S(2)}, u32[]{:S(2)}) async-start(bf16[2,16,16,512]{3,1,0,2:T(8,128)(2,1)} %bitcast.393), calls=%async_computation.3 | async-start | bytes 1048576 | tf_op jit(solution)/shard_map/all_to_all | solution.py:95
  64.4 210.8 %all-gather.6.cloned.1.call-start = ((), (), s32[]{:S(2)}) async-start(), calls=%async_computation.8 | async-start | bytes 17825792 | tf_op jit(solution)/shard_map/all_gather | solution.py:20
  64.6 16.6 %copy-start.17 = (f32[2,8,2]{1,0,2:T(2,128)}, f32[2,8,2]{1,0,2:T(2,128)S(1)}, u32[]{:S(2)}) copy-start(f32[2,8,2]{1,0,2:T(2,128)S(1)} %copy.264) | copy-start | bytes 388
  67.0 18.3 %copy-start.1 = (bf16[2,16,16,256]{3,1,2,0:T(8,128)(2,1)}, bf16[2,16,16,256]{3,1,2,0:T(8,128)(2,1)S(1)}, u32[]{:S(2)}) copy-start(bf16[2,16,16,256]{3,1,2,0:T(8,128)(2,1)S(1)} %copy.258) | copy-start | bytes 786436
  373.4 14.6 %all-to-all-start.7 = ((bf16[16,2,128]{2,1,0:T(2,128)(2,1)}), bf16[16,2,128]{2,1,0:T(2,128)(2,1)S(1)}, u32[]{:S(2)}, u32[]{:S(2)}) async-start(bf16[16,2,128]{2,1,0:T(2,128)(2,1)} %reshape.902), calls=%async_computation.7 | async-start | bytes 16384 | tf_op jit(solution)/shard_map/all_to_all | solution.py:161
  381.1 28.1 %copy-start.18 = (f32[2,8,2]{1,0,2:T(2,128)S(1)}, f32[2,8,2]{1,0,2:T(2,128)}, u32[]{:S(2)}) copy-start(f32[2,8,2]{1,0,2:T(2,128)} %copy-done.17) | copy-start | bytes 388
  381.1 28.3 %copy-start.16 = (pred[256,256]{1,0:T(8,128)(4,1)S(1)}, pred[256,256]{1,0:T(8,128)(4,1)}, u32[]{:S(2)}) copy-start(pred[256,256]{1,0:T(8,128)(4,1)} %iota_compare_fusion) | copy-start | bytes 196612
  381.1 28.3 %copy-start.20 = (f32[2,8,256]{2,1,0:T(8,128)S(1)}, f32[2,8,256]{2,1,0:T(8,128)}, u32[]{:S(2)}) copy-start(f32[2,8,256]{2,1,0:T(8,128)} %copy.293) | copy-start | bytes 49156
  381.1 28.3 %copy-start.22 = (f32[8]{0:T(128)S(1)}, f32[8]{0:T(128)}, u32[]{:S(2)}) copy-start(f32[8]{0:T(128)} %param.16) | copy-start | bytes 100
  384.9 12.0 %copy-start.6 = (f32[2,256,256]{2,1,0:T(8,128)S(1)}, f32[2,256,256]{2,1,0:T(8,128)}, u32[]{:S(2)}) copy-start(f32[2,256,256]{2,1,0:T(8,128)} %get-tuple-element.452) | copy-start | bytes 1572868
  388.0 17.7 %all-to-all-start.5 = ((bf16[2,256,1,256]{3,0,2,1:T(2,128)(2,1)}), bf16[2,256,1,256]{3,0,2,1:T(2,128)(2,1)S(1)}, u32[]{:S(2)}, u32[]{:S(2)}) async-start(bf16[2,256,1,256]{3,0,2,1:T(2,128)(2,1)} %copy.301), calls=%async_computation.5 | async-start | bytes 524288 | tf_op jit(solution)/shard_map/all_to_all | solution.py:159
  405.7 14.6 %all-to-all-start.6 = ((bf16[2,256,1,256]{3,0,2,1:T(2,128)(2,1)}), bf16[2,256,1,256]{3,0,2,1:T(2,128)(2,1)S(1)}, u32[]{:S(2)}, u32[]{:S(2)}) async-start(bf16[2,256,1,256]{3,0,2,1:T(2,128)(2,1)} %copy.305), calls=%async_computation.6 | async-start | bytes 524288 | tf_op jit(solution)/shard_map/all_to_all | solution.py:160
  409.4 16.6 %copy-start.8 = (f32[2,256,8]{2,0,1:T(2,128)S(1)}, f32[2,256,8]{2,0,1:T(2,128)}, u32[]{:S(2)}) copy-start(f32[2,256,8]{2,0,1:T(2,128)} %get-tuple-element.477) | copy-start | bytes 49156
  409.4 16.7 %copy-start.2 = (bf16[2,16,16,256]{3,1,2,0:T(8,128)(2,1)S(1)}, bf16[2,16,16,256]{3,1,2,0:T(8,128)(2,1)}, u32[]{:S(2)}) copy-start(bf16[2,16,16,256]{3,1,2,0:T(8,128)(2,1)} %copy-done.1) | copy-start | bytes 786436
  415.3 11.8 %copy-start = (bf16[2,256,1,8,64]{4,3,1,0,2:T(8,128)(2,1)S(1)}, bf16[2,256,1,8,64]{4,3,1,0,2:T(8,128)(2,1)}, u32[]{:S(2)}) copy-start(bf16[2,256,1,8,64]{4,3,1,0,2:T(8,128)(2,1)} %squeeze.85) | copy-start | bytes 1572868
  421.0 21.2 %all-to-all-start.4 = ((bf16[2,256,1,512]{3,0,2,1:T(2,128)(2,1)}), bf16[2,256,1,512]{3,0,2,1:T(2,128)(2,1)S(1)}, u32[]{:S(2)}, u32[]{:S(2)}) async-start(bf16[2,256,1,512]{3,0,2,1:T(2,128)(2,1)} %copy.294), calls=%async_computation.4 | async-start | bytes 1048576 | tf_op jit(solution)/shard_map/all_to_all | solution.py:158
  (9 other events, 30.6 us)
Sparse Core Ops, SparseCore 0:
  45.8 110.8 all-gather.7
  159.1 116.0 all-gather.5
where the time goes:
time: 453 us; the launch traced here: 450 us
  waiting for transfers between devices  221 us (49%)
  other arithmetic  58.4 us (13%)
  local copies, waits for them, and re-layouts  56.3 us (12%)
  starting transfers between devices  41.1 us (9%)
  matrix products  40.7 us (9%)
  blocking collectives  18 us (4%)
  between operations  14.5 us (3%)
    all_gather x2, waiting for transfers between devices, prefix(): gathered = jax.tree.map(lambda a: lax.all_gather(a, axis), part)  169 us
    add x15, other arithmetic, link_states(): jnp.exp(later[0])[..., None, None] * earlier[1] + later[1]  22.2 us
    dot_general x3, matrix products, stretched_step_update(): within = jnp.einsum('jetu,ujep->tjep', mixing, x_vals, precision=highest)  18.3 us
    all_gather x1, blocking collectives, prefix(): gathered = jax.tree.map(lambda a: lax.all_gather(a, axis), part)  18 us
    another operation x9, other arithmetic  15.6 us
    another operation x23, local copies, waits for them, and re-layouts  14.7 us
    all_to_all x1, waiting for transfers between devices, on_device(): lax.all_to_all(by_part(x_in, heads_dev * HEAD_DIM), 'head', split_axis=2,...  14.2 us
    dot_general x3, matrix products, carry_state(): jnp.einsum('tjep,tjn->jepn', x_vals * weight[..., None], b_vals, precisio...  10.1 us
  transfers between devices with their start and end apart: 10, of which 10 were waited for; matrix products, arithmetic and copies ran while one was open for 11% of the time, Pallas kernels for 0%

commit v1 on v0

v1 whole, which is shorter than its diff:
```python
from types import SimpleNamespace

import jax
import jax.numpy as jnp
from jax import lax
from jax.experimental import pallas as pl
from jax.experimental.pallas import tpu as pltpu
from jax.sharding import PartitionSpec as P

HEAD_DIM = 64
STATE = 256
STRETCH = 256
LANES = 128
MESH = pl.DeviceIdType.MESH
F32 = jnp.float32
BF16 = jnp.bfloat16
NN = (((1,), (0,)), ((), ()))
NT = (((1,), (1,)), ((), ()))
TN = (((0,), (0,)), ((), ()))


def dot(a, b, dims=NN):
    return lax.dot_general(a, b, dims, preferred_element_type=F32)


def split(value, count):
    parts = []
    for _ in range(count):
        part = value.astype(BF16)
        parts.append(part)
        value = value - part.astype(F32)
    return parts


def dot_split(a, b, dims=NN):
    a_parts = [a] if a.dtype == BF16 else split(a, 2)
    b_parts = [b] if b.dtype == BF16 else split(b, 2)
    total = dot(a_parts[0], b_parts[0], dims)
    for i, left in enumerate(a_parts):
        for j, right in enumerate(b_parts):
            if i + j == 1:
                total = total + dot(left, right, dims)
    return total


def times_exact(value, ones):
    first, second, third = split(value, 3)
    return dot(first, ones) + (dot(second, ones) + dot(third, ones))


def exact_times(ones, value):
    first, second, third = split(value, 3)
    return dot(ones, first) + (dot(ones, second) + dot(ones, third))


def iota(shape, axis):
    return lax.broadcasted_iota(jnp.int32, shape, axis)


def one_hot(condition):
    return jnp.where(condition, 1.0, 0.0).astype(BF16)


def mixer(dims, names, *refs):
    r = SimpleNamespace(**dict(zip(names, refs)))
    ns, nh, seqs, rows, heads = dims
    width = heads * HEAD_DIM
    part = STATE // ns
    chips = nh // 2
    s, h = lax.axis_index("seq"), lax.axis_index("head")
    core = lax.rem(h, 2)
    chip = h // 2
    other = (s, h + 1 - 2 * core)

    def head_peer(k):
        return lax.rem(h + k, nh)

    def seq_peer(k):
        return lax.rem(s + k, ns)

    def remote(src, dst, sem, device):
        pltpu.make_async_remote_copy(
            src, dst, r.send_sem.at[sem], r.recv_sem.at[sem], device_id=device, device_id_type=MESH
        ).start()

    def local(src, dst, sem):
        copy = pltpu.make_async_copy(src, dst, r.local_sem.at[sem])
        copy.start()
        return copy

    def arrived(ref, sem):
        pltpu.make_async_copy(ref, ref, r.recv_sem.at[sem]).wait()

    def left(ref, sem):
        pltpu.make_async_copy(ref, ref, r.send_sem.at[sem]).wait()

    def over(count, body, start=0, step=1):
        def one(i, carry):
            body(start + i * step)
            return carry

        lax.fori_loop(0, count, one, 0)

    def columns(index, size):
        return pl.ds(pl.multiple_of(index * size, size), size)

    DT, C, C2, B, B2, TOT = range(6)
    X, G, D, F, S, GX, GB, GC, GD = (6 + seqs * i for i in range(9))

    barrier = pltpu.get_barrier_semaphore()

    def greet_head(k):
        pl.semaphore_signal(barrier, inc=1, device_id=(s, head_peer(k)), device_id_type=MESH)

    def greet_seq(k):
        pl.semaphore_signal(barrier, inc=1, device_id=(seq_peer(k), h), device_id_type=MESH)

    over(nh - 1, greet_head, 1)
    over(ns - 1, greet_seq, 1)

    own = [
        local(r.dt_in, r.dt_all.at[:, h], 0),
        local(r.c_in.at[:, :, columns(chip, STATE)], r.c_all.at[:, chip, core], 1),
        local(r.b_in.at[:, :, columns(chip, STATE)], r.b_all.at[:, chip, core], 2),
        local(r.x_in.at[:, :, columns(h, width)], r.x_all.at[:, h], 3),
        local(r.gy_in, r.gy, 4),
    ]

    pl.semaphore_wait(barrier, nh - 1 + ns - 1)

    def send_dt(k):
        remote(r.dt_in, r.dt_all.at[:, h], DT, (s, head_peer(k)))

    def send_c(k):
        peer = head_peer(k)
        remote(r.c_in.at[:, :, columns(peer // 2, STATE)], r.c_all.at[:, chip, core], C, (s, peer))

    def send_b(k):
        peer = head_peer(k)
        remote(r.b_in.at[:, :, columns(peer // 2, STATE)], r.b_all.at[:, chip, core], B, (s, peer))

    over(nh - 1, send_dt, 1)
    over(chips - 1, send_c, 2, 2)
    over(chips - 1, send_b, 2, 2)
    for q in range(seqs):

        def send_x(k, q=q):
            peer = head_peer(k)
            remote(r.x_in.at[q, :, columns(peer, width)], r.x_all.at[q, h], X + q, (s, peer))

        over(nh - 1, send_x, 1)

    lane_row = iota((1, LANES), 1)
    rate = jnp.zeros((1, LANES), F32)
    skip_row = jnp.zeros((1, width), F32)
    wide_row = iota((1, width), 1) // HEAD_DIM
    for e in range(heads):
        rate = jnp.where(lane_row == e, r.a_log[e], rate)
        skip_row = jnp.where(wide_row == e, r.skip[e], skip_row)
    rate = jnp.where(lane_row < heads, -jnp.exp(rate), 0.0)
    spread = one_hot(iota((LANES, width), 0) == iota((LANES, width), 1) // HEAD_DIM)
    gather = one_hot(iota((width, LANES), 0) // HEAD_DIM == iota((width, LANES), 1))
    causal = iota((STRETCH, STRETCH), 0) >= iota((STRETCH, STRETCH), 1)
    lower = one_hot(causal)
    upper = one_hot(iota((STRETCH, STRETCH), 0) <= iota((STRETCH, STRETCH), 1))

    own[0].wait()
    arrived(r.dt_all.at[:, 0 : nh - 1], DT)
    all_heads = r.dt_all.shape[3]
    pick_at = (all_heads, LANES)
    pick = one_hot((iota(pick_at, 0) == h * heads + iota(pick_at, 1)) & (iota(pick_at, 1) < heads))
    r.tot_send[...] = jnp.zeros_like(r.tot_send)
    for q in range(seqs):
        raw = dot(r.dt_all[q].reshape(STRETCH, all_heads), pick)
        dt = jnp.maximum(raw, 0.0) + jnp.log1p(jnp.exp(-jnp.abs(raw)))
        cum = exact_times(lower, dt * rate)
        last = cum[STRETCH - 1 :, :]
        r.raw[q] = raw
        r.dt[q] = dt
        r.tot_send[pl.ds(q, 1), :] = last
        r.w_wide[q] = times_exact(jnp.exp(last - cum) * dt, spread)
        r.e_wide[q] = times_exact(jnp.exp(cum), spread)
        r.u_row[q] = jnp.transpose(cum - jnp.log(dt))[:heads, :]
        for e in range(heads):
            r.cum_col[q, e] = jnp.broadcast_to(cum[:, e : e + 1], (STRETCH, LANES))

    def send_tot(k):
        remote(r.tot_send, r.tot_all.at[s], TOT, (seq_peer(k), h))

    over(ns - 1, send_tot, 1)
    r.tot_all[s] = r.tot_send[...]

    own[4].wait()
    own[1].wait()
    arrived(r.c_all.at[:, 0 : chips - 1, 0], C)
    remote(r.c_all.at[:, :, core], r.c_all.at[:, :, core], C2, other)
    for q in range(seqs):
        first, second = split(r.gy[q].astype(F32) * r.e_wide[q], 2)
        r.gys_hi[q] = first
        r.gys_lo[q] = second
        r.gy_t[q] = jnp.transpose(r.gy[q])
    arrived(r.c_all.at[:, :, 0], C2)

    def c_of(q):
        return r.c_all[q].reshape(STRETCH, STATE)

    def b_of(q):
        return r.b_all[q].reshape(STRETCH, STATE)

    def x_of(q):
        return r.x_all[q].reshape(STRETCH, width)

    def send_parts(q, source, target, sem):
        def one(k):
            peer = seq_peer(k)
            remote(source.at[q, columns(peer, part), :], target.at[q, s], sem + q, (peer, h))

        over(ns - 1, one, 1)
        target[q, s] = source[q, columns(s, part), :]

    for q in range(seqs):
        r.g_out[q] = dot(c_of(q), r.gys_hi[q], TN) + dot(c_of(q), r.gys_lo[q], TN)
        send_parts(q, r.g_out, r.g_in, G)

    own[2].wait()
    arrived(r.b_all.at[:, 0 : chips - 1, 0], B)
    remote(r.b_all.at[:, :, core], r.b_all.at[:, :, core], B2, other)
    arrived(r.b_all.at[:, :, 0], B2)

    def decays(q):
        r.scores[q] = dot(c_of(q), b_of(q), NT)

        def one(e):
            column = r.cum_col[q, e]
            gap = jnp.concatenate([column, column], axis=1) - r.u_row[q, pl.ds(e, 1), :]
            decay = jnp.where(causal, jnp.exp(gap), 0.0)
            r.decay[q, e] = decay
            first, second = split(r.scores[q] * decay, 2)
            r.mix_hi[q, e] = first
            r.mix_lo[q, e] = second
            rows_e = columns(e, HEAD_DIM)
            grad = r.gy_t[q, rows_e, :]
            r.z_t[q, rows_e, :] = dot(grad, first) + dot(grad, second)

        over(heads, one)

    def send_state(q):
        arrived(r.x_all.at[q, 0 : nh - 1], X + q)
        first, second = split(x_of(q).astype(F32) * r.w_wide[q], 2)
        r.xs_hi[q] = first
        r.xs_lo[q] = second
        r.f_out[q] = dot(b_of(q), first, TN) + dot(b_of(q), second, TN)
        send_parts(q, r.f_out, r.f_in, F)

    def within(q):
        r.d_scores[q] = jnp.zeros((STRETCH, STRETCH), F32)
        low = iota((STRETCH, LANES), 1) < HEAD_DIM

        def one(i):
            cols = columns(i, LANES)
            x_pair = r.x_all[q, :, :, cols].reshape(STRETCH, LANES)
            grad = r.gy[q, :, cols].astype(F32)
            results = []
            total = r.d_scores[q]
            for k in range(2):
                e = 2 * i + k
                results.append(dot(r.mix_hi[q, e], x_pair) + dot(r.mix_lo[q, e], x_pair))
                masked = jnp.where(low if k == 0 else ~low, grad, 0.0).astype(BF16)
                total = total + dot(masked, x_pair, NT) * r.decay[q, e]
            r.d_scores[q] = total
            r.y_in[q, :, cols] = jnp.where(low, results[0], results[1])

        over(heads // 2, one)

    def scan(q, source, result, target, sem, sem_in, reverse):
        arrived(source.at[q, 0 : ns - 1], sem_in + q)

        def one(i, state):
            block = ns - 1 - i if reverse else i
            result[q, block] = state
            return r.factor[pl.ds(block * 8 + q, 1), :] * state + source[q, block]

        lax.fori_loop(0, ns, one, jnp.zeros((part, width), F32))

        def back(k):
            peer = seq_peer(k)
            remote(result.at[q, peer], target.at[q, columns(s, part), :], sem + q, (peer, h))

        over(ns - 1, back, 1)
        target[q, columns(s, part), :] = result[q, s]

    def states_here(q, target, sem):
        arrived(target.at[q, 0 : (ns - 1) * part, :], sem + q)

    def send_rows(q, source, target_of, sem):
        def one(k):
            peer = head_peer(k)
            remote(source.at[q, columns(peer, rows), :], target_of(q), sem + q, (s, peer))

        over(nh - 1, one, 1)

    def gx_slot(q):
        return r.gx_out.at[q, :, columns(h, width)]

    own_gx = []

    def grad_x(q):
        states_here(q, r.d_all, D)
        r.xc[q] = r.w_wide[q] * dot_split(b_of(q), r.d_all[q])
        r.xp[q] = jnp.transpose(r.z_t[q]) + r.xc[q]
        r.gx[q] = (skip_row * r.gy[q].astype(F32) + r.xp[q]).astype(BF16)
        send_rows(q, r.gx, gx_slot, GX)
        own_gx.append(local(r.gx.at[q, columns(h, rows), :], gx_slot(q), 5 + q))

    def grad_b(q):
        first, second = split(jnp.transpose(r.d_scores[q]), 2)
        value = dot(first, c_of(q)) + dot(second, c_of(q))
        d_hi, d_lo = split(r.d_all[q], 2)
        value = value + dot(r.xs_hi[q], d_hi, NT)
        value = value + (dot(r.xs_hi[q], d_lo, NT) + dot(r.xs_lo[q], d_hi, NT))
        r.gb[q] = value.astype(BF16)
        send_rows(q, r.gb, lambda q: r.gb_all.at[q, h], GB)
        r.gb_all[q, h] = r.gb[q, columns(h, rows), :]

    own_y = []

    def finish(q):
        states_here(q, r.s_all, S)
        s_hi, s_lo = split(r.s_all[q], 2)
        first, second = split(r.d_scores[q], 2)
        value = dot(first, b_of(q)) + dot(second, b_of(q))
        value = value + dot(r.gys_hi[q], s_hi, NT)
        value = value + (dot(r.gys_hi[q], s_lo, NT) + dot(r.gys_lo[q], s_hi, NT))
        r.gc[q] = value.astype(BF16)
        send_rows(q, r.gc, lambda q: r.gc_all.at[q, h], GC)
        r.gc_all[q, h] = r.gc[q, columns(h, rows), :]

        y = r.y_in[q] + r.e_wide[q] * (dot(c_of(q), s_hi) + dot(c_of(q), s_lo))
        x = x_of(q).astype(F32)
        r.y[q] = (y + skip_row * x).astype(BF16)
        own_y.append(local(r.y.at[q], r.y_out.at[q], 5 + seqs + q))

        dt = r.dt[q]
        v = times_exact(x * r.xp[q], gather)
        d_cum = times_exact(r.gy[q].astype(F32) * y, gather) - v
        at_last = jnp.sum(x * r.xc[q], axis=0, keepdims=True) + r.e_wide[q, STRETCH - 1 :, :] * jnp.sum(
            r.s_all[q] * r.d_all[q], axis=0, keepdims=True
        )
        at_last = times_exact(jnp.broadcast_to(at_last, (8, width)), gather)[:1]
        d_sum = exact_times(upper, d_cum) + at_last
        grad = (v / dt + rate * d_sum) * jax.nn.sigmoid(r.raw[q])
        r.gd[q] = grad.astype(BF16)
        send_rows(q, r.gd, lambda q: r.gd_all.at[q, h], GD)
        r.gd_all[q, h] = r.gd[q, columns(h, rows), :]

    for q in range(seqs):
        decays(q)
    own[3].wait()
    send_state(0)
    arrived(r.tot_all.at[0 : ns - 1], TOT)
    r.factor[...] = jnp.exp(times_exact(r.tot_all[...].reshape(ns * 8, LANES), spread))
    scan(0, r.g_in, r.g_res, r.d_all, D, G, True)
    within(0)
    send_state(1)
    scan(1, r.g_in, r.g_res, r.d_all, D, G, True)
    grad_x(0)
    scan(0, r.f_in, r.f_res, r.s_all, S, F, False)
    within(1)
    grad_b(0)
    grad_x(1)
    scan(1, r.f_in, r.f_res, r.s_all, S, F, False)
    grad_b(1)
    finish(0)
    finish(1)

    for q in range(seqs):
        arrived(r.gb_all.at[q, 0 : nh - 1], GB + q)
        for g in range(chips):
            both = r.gb_all[q, 2 * g].astype(F32) + r.gb_all[q, 2 * g + 1].astype(F32)
            r.gb_out[q, :, g * STATE : (g + 1) * STATE] = both.astype(BF16)
    for q in range(seqs):
        arrived(r.gc_all.at[q, 0 : nh - 1], GC + q)
        for g in range(chips):
            both = r.gc_all[q, 2 * g].astype(F32) + r.gc_all[q, 2 * g + 1].astype(F32)
            r.gc_out[q, :, g * STATE : (g + 1) * STATE] = both.astype(BF16)
    place_at = (LANES, all_heads)
    for q in range(seqs):
        arrived(r.gd_all.at[q, 0 : nh - 1], GD + q)
        total = jnp.zeros((rows, all_heads), F32)
        for p in range(nh):
            place = one_hot((iota(place_at, 1) == p * heads + iota(place_at, 0)) & (iota(place_at, 0) < heads))
            total = total + dot(r.gd_all[q, p], place)
        r.gdt_out[q] = total.astype(BF16)
    for q in range(seqs):
        arrived(r.gx_out.at[q, :, 0 : (nh - 1) * width], GX + q)

    left(r.dt_all.at[:, 0 : nh - 1], DT)
    left(r.c_all.at[:, 0 : chips - 1, 0], C)
    left(r.c_all.at[:, :, 0], C2)
    left(r.b_all.at[:, 0 : chips - 1, 0], B)
    left(r.b_all.at[:, :, 0], B2)
    left(r.tot_all.at[0 : ns - 1], TOT)
    for q in range(seqs):
        left(r.x_all.at[q, 0 : nh - 1], X + q)
        left(r.g_in.at[q, 0 : ns - 1], G + q)
        left(r.g_res.at[q, 0 : ns - 1], D + q)
        left(r.f_in.at[q, 0 : ns - 1], F + q)
        left(r.f_res.at[q, 0 : ns - 1], S + q)
        left(r.gx.at[q, 0 : (nh - 1) * rows, :], GX + q)
        left(r.gb_all.at[q, 0 : nh - 1], GB + q)
        left(r.gc_all.at[q, 0 : nh - 1], GC + q)
        left(r.gd_all.at[q, 0 : nh - 1], GD + q)
    for copy in own_gx + own_y:
        copy.wait()


def on_device(x_in, b_in, c_in, dt_in, a_log, skip_gain, grad_y):
    ns, nh = lax.axis_size("seq"), lax.axis_size("head")
    seqs, rows, all_heads = dt_in.shape
    heads = a_log.shape[0]
    width = heads * HEAD_DIM
    part = STATE // ns
    chips = nh // 2
    scratch = {
        "dt_all": ((seqs, nh, rows, all_heads), BF16),
        "c_all": ((seqs, chips, 2, rows, STATE), BF16),
        "b_all": ((seqs, chips, 2, rows, STATE), BF16),
        "x_all": ((seqs, nh, rows, width), BF16),
        "gy": ((seqs, STRETCH, width), BF16),
        "gy_t": ((seqs, width, STRETCH), BF16),
        "raw": ((seqs, STRETCH, LANES), F32),
        "dt": ((seqs, STRETCH, LANES), F32),
        "tot_send": ((8, LANES), F32),
        "tot_all": ((ns, 8, LANES), F32),
        "factor": ((ns * 8, width), F32),
        "w_wide": ((seqs, STRETCH, width), F32),
        "e_wide": ((seqs, STRETCH, width), F32),
        "u_row": ((seqs, heads, STRETCH), F32),
        "cum_col": ((seqs, heads, STRETCH, LANES), F32),
        "gys_hi": ((seqs, STRETCH, width), BF16),
        "gys_lo": ((seqs, STRETCH, width), BF16),
        "xs_hi": ((seqs, STRETCH, width), BF16),
        "xs_lo": ((seqs, STRETCH, width), BF16),
        "scores": ((seqs, STRETCH, STRETCH), F32),
        "d_scores": ((seqs, STRETCH, STRETCH), F32),
        "decay": ((seqs, heads, STRETCH, STRETCH), F32),
        "mix_hi": ((seqs, heads, STRETCH, STRETCH), BF16),
        "mix_lo": ((seqs, heads, STRETCH, STRETCH), BF16),
        "z_t": ((seqs, width, STRETCH), F32),
        "xc": ((seqs, STRETCH, width), F32),
        "xp": ((seqs, STRETCH, width), F32),
        "y_in": ((seqs, STRETCH, width), F32),
        "y": ((seqs, STRETCH, width), BF16),
        "gx": ((seqs, STRETCH, width), BF16),
        "gb": ((seqs, STRETCH, STATE), BF16),
        "gc": ((seqs, STRETCH, STATE), BF16),
        "gd": ((seqs, STRETCH, LANES), BF16),
        "gb_all": ((seqs, nh, rows, STATE), BF16),
        "gc_all": ((seqs, nh, rows, STATE), BF16),
        "gd_all": ((seqs, nh, rows, LANES), BF16),
    }
    for name in ("g", "f"):
        scratch[name + "_out"] = ((seqs, STATE, width), F32)
        scratch[name + "_in"] = ((seqs, ns, part, width), F32)
        scratch[name + "_res"] = ((seqs, ns, part, width), F32)
    for name in ("d_all", "s_all"):
        scratch[name] = ((seqs, STATE, width), F32)
    sems = 6 + 9 * seqs
    names = (
        ["a_log", "skip", "x_in", "b_in", "c_in", "dt_in", "gy_in"]
        + ["y_out", "gx_out", "gb_out", "gc_out", "gdt_out"]
        + list(scratch)
        + ["send_sem", "recv_sem", "local_sem"]
    )
    dims = (ns, nh, seqs, rows, heads)

    def body(*refs):
        mixer(dims, names, *refs)

    anywhere = pl.BlockSpec(memory_space=pl.ANY)
    small = pl.BlockSpec(memory_space=pltpu.SMEM)
    vmem = pl.BlockSpec(memory_space=pltpu.VMEM)

    def like(array):
        return jax.ShapeDtypeStruct(array.shape, BF16)

    return pl.pallas_call(
        body,
        out_shape=(like(grad_y), like(x_in), like(b_in), like(c_in), like(dt_in)),
        in_specs=[small, small] + [anywhere] * 5,
        out_specs=(anywhere, anywhere, vmem, vmem, vmem),
        scratch_shapes=[pltpu.VMEM(shape, dtype) for shape, dtype in scratch.values()]
        + [
            pltpu.SemaphoreType.DMA((sems,)),
            pltpu.SemaphoreType.DMA((sems,)),
            pltpu.SemaphoreType.DMA((5 + 2 * seqs,)),
        ],
        compiler_params=pltpu.CompilerParams(
            collective_id=0, has_side_effects=True, vmem_limit_bytes=56 * 1024 * 1024
        ),
        name="mixer",
    )(a_log, skip_gain, x_in, b_in, c_in, dt_in, grad_y)


def solution(mesh):
    spread = P(None, ("seq", "head"), None)
    return jax.shard_map(
        on_device,
        mesh=mesh,
        in_specs=(spread, spread, spread, spread, P("head"), P("head"), P(None, "seq", "head")),
        out_specs=(P(None, "seq", "head"), spread, spread, spread, spread),
        check_vma=False,
    )
```

time: 453 us -> 87.5 us (0.19)
  the two profiles are of different devices: /device:TPU:31 before, /device:TPU:1 now
where the time goes in v1:
time: 87.5 us; the launch traced here: 87.3 us
  Pallas kernels  81.5 us (93%)
  local copies, waits for them, and re-layouts  5.2 us (6%)
    pallas_call x1, Pallas kernels, on_device(): pl.pallas_call(body, out_shape=(like(grad_y), like(x_in), like(b_in), lik...  81.5 us
    unnamed x13, local copies, waits for them, and re-layouts  5.2 us

profile of v1, /device:TPU:1, one launch (start us, length us, event | category | flops | bytes accessed | tf_op | source)
XLA Modules:
  0.0 87.3 jit_solution(641103285305628572)
XLA Ops:
  0.6 81.5 %mixer.1 = (bf16[2,256,512]{2,1,0:T(8,128)(2,1)}, bf16[2,16,8192]{2,1,0:T(8,128)(2,1)}, bf16[2,16,2048]{2,1,0:T(8,128)(2,1)}, bf16[2,16,2048]{2,1,0:T(8,128)(2,1)}, bf16[2,16,128]{2,1,0:T(8,128)(2,1)}) custom-call(f32[8]{0:T(128)} %refs_0_.1, f32[8]{0:T(128)} %refs_1_.1, bf16[2,16,8192]{2,1,0:T(8,128)(2,1)} %refs_2_.1, bf16[2,16,2048]{2,1,0:T(8,128)(2,1)} %refs_3_.1, ...), custom_call_target="tpu_custom_call" | custom-call | tf_op jit(solution)/shard_map/mixer/pallas_call | solution.py:487
  82.1 0.0 copy-start
  82.1 1.9 %copy.17 = bf16[2,256,512]{2,1,0:T(8,128)(2,1)} copy(bf16[2,256,512]{2,1,0:T(8,128)(2,1)} %get-tuple-element.10) | data formatting | bytes 1048576
  84.0 0.0 copy-done
  84.0 0.0 copy-start.2
  84.0 0.8 copy.18
  84.8 0.2 copy-done.2
  85.1 0.0 copy-start.1
  85.1 0.7 copy.19
  85.7 0.3 copy-done.1
  86.0 0.0 copy-start.3
  86.0 0.7 copy.20
  86.7 0.0 copy-done.3
  86.7 0.6 copy.21
Async XLA Ops:
  82.1 1.9 %copy-start = (bf16[2,16,8192]{2,1,0:T(8,128)(2,1)S(1)}, bf16[2,16,8192]{2,1,0:T(8,128)(2,1)}, u32[]{:S(2)}) copy-start(bf16[2,16,8192]{2,1,0:T(8,128)(2,1)} %get-tuple-element.11) | copy-start | bytes 1572868
  84.0 1.0 %copy-start.2 = (bf16[2,16,2048]{2,1,0:T(8,128)(2,1)S(1)}, bf16[2,16,2048]{2,1,0:T(8,128)(2,1)}, u32[]{:S(2)}) copy-start(bf16[2,16,2048]{2,1,0:T(8,128)(2,1)} %get-tuple-element.12) | copy-start | bytes 393220
  85.1 1.0 %copy-start.1 = (bf16[2,16,2048]{2,1,0:T(8,128)(2,1)S(1)}, bf16[2,16,2048]{2,1,0:T(8,128)(2,1)}, u32[]{:S(2)}) copy-start(bf16[2,16,2048]{2,1,0:T(8,128)(2,1)} %get-tuple-element.13) | copy-start | bytes 393220
  86.0 0.7 copy-start.3

commit v2 on v1

--- a/solution.py
+++ b/solution.py
@@ -17,6 +17,11 @@
 NN = (((1,), (0,)), ((), ()))
 NT = (((1,), (1,)), ((), ()))
 TN = (((0,), (0,)), ((), ()))
+LN2 = 0.6931471805599453
+TINY = 1e-30
+CODE_SPAN = 252.0
+X_B = 6.0 * 6.0 * 1.001
+GY_C = 4.0 * 0.375 * 1.001
 
 
 def dot(a, b, dims=NN):
@@ -51,6 +56,22 @@
 def exact_times(ones, value):
     first, second, third = split(value, 3)
     return dot(ones, first) + (dot(ones, second) + dot(ones, third))
+
+
+def encode(value, bound):
+    share = jnp.maximum(jnp.abs(value) / jnp.maximum(bound, TINY), TINY)
+    level = jnp.exp2(jnp.log(share) * (0.125 / LN2))
+    code = jnp.exp2(level * CODE_SPAN - 0.5 * CODE_SPAN)
+    return jnp.where(value < 0.0, -code, code).astype(BF16)
+
+
+def decode(code, bound):
+    code = code.astype(F32)
+    level = jnp.maximum(jnp.log(jnp.abs(code)) * (1.0 / (LN2 * CODE_SPAN)) + 0.5, 0.0)
+    square = level * level
+    square = square * square
+    size = square * square * bound
+    return jnp.where(code < 0.0, -size, size)
 
 
 def iota(shape, axis):
@@ -104,8 +125,8 @@
     def columns(index, size):
         return pl.ds(pl.multiple_of(index * size, size), size)
 
-    DT, C, C2, B, B2, TOT = range(6)
-    X, G, D, F, S, GX, GB, GC, GD = (6 + seqs * i for i in range(9))
+    DT, C, C2, B, B2, TOT, GD = range(7)
+    X, G, D, F, S, GX, GB, GC, GB2, GC2 = (7 + seqs * i for i in range(10))
 
     barrier = pltpu.get_barrier_semaphore()
 
@@ -119,17 +140,31 @@
     over(ns - 1, greet_seq, 1)
 
     own = [
-        local(r.dt_in, r.dt_all.at[:, h], 0),
-        local(r.c_in.at[:, :, columns(chip, STATE)], r.c_all.at[:, chip, core], 1),
-        local(r.b_in.at[:, :, columns(chip, STATE)], r.b_all.at[:, chip, core], 2),
-        local(r.x_in.at[:, :, columns(h, width)], r.x_all.at[:, h], 3),
-        local(r.gy_in, r.gy, 4),
+        local(r.c_in.at[:, :, columns(chip, STATE)], r.c_all.at[:, chip, core], 0),
+        local(r.b_in.at[:, :, columns(chip, STATE)], r.b_all.at[:, chip, core], 1),
+        local(r.x_in.at[:, :, columns(h, width)], r.x_all.at[:, h], 2),
+        local(r.gy_in, r.gy, 3),
     ]
 
+    all_heads = r.dt_in.shape[2]
+    pack_lane = iota((rows, all_heads), 1)
+    raw_dt = [r.dt_in[q].astype(F32) for q in range(seqs)]
+    for p in range(nh):
+        packed = jnp.zeros((rows, all_heads), F32)
+        for q in range(seqs):
+            moved = pltpu.roll(raw_dt[q], (q - p) * heads % all_heads, 1)
+            packed = jnp.where(pack_lane // heads == q, moved, packed)
+        r.dt_pack[p] = packed.astype(BF16)
+    r.dt_all[h] = r.dt_pack[h]
+    own[3].wait()
+    for q in range(seqs):
+        r.gy_t[q] = jnp.transpose(r.gy[q])
+
     pl.semaphore_wait(barrier, nh - 1 + ns - 1)
 
     def send_dt(k):
-        remote(r.dt_in, r.dt_all.at[:, h], DT, (s, head_peer(k)))
+        peer = head_peer(k)
+        remote(r.dt_pack.at[peer], r.dt_all.at[h], DT, (s, peer))
 
     def send_c(k):
         peer = head_peer(k)
@@ -164,22 +199,23 @@
     lower = one_hot(causal)
     upper = one_hot(iota((STRETCH, STRETCH), 0) <= iota((STRETCH, STRETCH), 1))
 
-    own[0].wait()
-    arrived(r.dt_all.at[:, 0 : nh - 1], DT)
-    all_heads = r.dt_all.shape[3]
-    pick_at = (all_heads, LANES)
-    pick = one_hot((iota(pick_at, 0) == h * heads + iota(pick_at, 1)) & (iota(pick_at, 1) < heads))
+    arrived(r.dt_all.at[0 : nh - 1], DT)
+    raw_all = r.dt_all[...].reshape(STRETCH, all_heads).astype(F32)
     r.tot_send[...] = jnp.zeros_like(r.tot_send)
     for q in range(seqs):
-        raw = dot(r.dt_all[q].reshape(STRETCH, all_heads), pick)
+        raw = raw_all if q == 0 else pltpu.roll(raw_all, all_heads - q * heads, 1)
         dt = jnp.maximum(raw, 0.0) + jnp.log1p(jnp.exp(-jnp.abs(raw)))
         cum = exact_times(lower, dt * rate)
         last = cum[STRETCH - 1 :, :]
         r.raw[q] = raw
         r.dt[q] = dt
+        weight = jnp.exp(last - cum) * dt
+        growth = jnp.exp(cum)
         r.tot_send[pl.ds(q, 1), :] = last
-        r.w_wide[q] = times_exact(jnp.exp(last - cum) * dt, spread)
-        r.e_wide[q] = times_exact(jnp.exp(cum), spread)
+        r.tot_send[pl.ds(seqs + q, 1), :] = X_B * jnp.sum(weight, axis=0, keepdims=True)
+        r.tot_send[pl.ds(2 * seqs + q, 1), :] = GY_C * jnp.sum(growth, axis=0, keepdims=True)
+        r.w_wide[q] = times_exact(weight, spread)
+        r.e_wide[q] = times_exact(growth, spread)
         r.u_row[q] = jnp.transpose(cum - jnp.log(dt))[:heads, :]
         for e in range(heads):
             r.cum_col[q, e] = jnp.broadcast_to(cum[:, e : e + 1], (STRETCH, LANES))
@@ -189,16 +225,21 @@
 
     over(ns - 1, send_tot, 1)
     r.tot_all[s] = r.tot_send[...]
-
-    own[4].wait()
-    own[1].wait()
+    r.own_wide[...] = times_exact(r.tot_send[...], spread)
+
+    def own_bound(row):
+        return r.own_wide[pl.ds(row, 1), :]
+
+    own[0].wait()
     arrived(r.c_all.at[:, 0 : chips - 1, 0], C)
     remote(r.c_all.at[:, :, core], r.c_all.at[:, :, core], C2, other)
     for q in range(seqs):
         first, second = split(r.gy[q].astype(F32) * r.e_wide[q], 2)
         r.gys_hi[q] = first
         r.gys_lo[q] = second
-        r.gy_t[q] = jnp.transpose(r.gy[q])
+    own[1].wait()
+    arrived(r.b_all.at[:, 0 : chips - 1, 0], B)
+    remote(r.b_all.at[:, :, core], r.b_all.at[:, :, core], B2, other)
     arrived(r.c_all.at[:, :, 0], C2)
 
     def c_of(q):
@@ -219,12 +260,10 @@
         target[q, s] = source[q, columns(s, part), :]
 
     for q in range(seqs):
-        r.g_out[q] = dot(c_of(q), r.gys_hi[q], TN) + dot(c_of(q), r.gys_lo[q], TN)
+        state = dot(c_of(q), r.gys_hi[q], TN) + dot(c_of(q), r.gys_lo[q], TN)
+        r.g_out[q] = encode(state, own_bound(2 * seqs + q))
         send_parts(q, r.g_out, r.g_in, G)
 
-    own[2].wait()
-    arrived(r.b_all.at[:, 0 : chips - 1, 0], B)
-    remote(r.b_all.at[:, :, core], r.b_all.at[:, :, core], B2, other)
     arrived(r.b_all.at[:, :, 0], B2)
 
     def decays(q):
@@ -249,7 +288,8 @@
         first, second = split(x_of(q).astype(F32) * r.w_wide[q], 2)
         r.xs_hi[q] = first
         r.xs_lo[q] = second
-        r.f_out[q] = dot(b_of(q), first, TN) + dot(b_of(q), second, TN)
+        state = dot(b_of(q), first, TN) + dot(b_of(q), second, TN)
+        r.f_out[q] = encode(state, own_bound(seqs + q))
         send_parts(q, r.f_out, r.f_in, F)
 
     def within(q):
@@ -272,15 +312,22 @@
 
         over(heads // 2, one)
 
-    def scan(q, source, result, target, sem, sem_in, reverse):
+    def scan(q, source, result, bounds, target, sem, sem_in, bound_row, reverse):
         arrived(source.at[q, 0 : ns - 1], sem_in + q)
 
-        def one(i, state):
+        def wide(block, row):
+            return r.wide[pl.ds(block * 8 + row, 1), :]
+
+        def one(i, carry):
             block = ns - 1 - i if reverse else i
-            result[q, block] = state
-            return r.factor[pl.ds(block * 8 + q, 1), :] * state + source[q, block]
-
-        lax.fori_loop(0, ns, one, jnp.zeros((part, width), F32))
+            state, bound = carry
+            bounds[q, block] = bound
+            result[q, block] = encode(state, bound)
+            factor = jnp.exp(wide(block, q))
+            block_bound = wide(block, bound_row + q)
+            return (factor * state + decode(source[q, block], block_bound), factor * bound + block_bound)
+
+        lax.fori_loop(0, ns, one, (jnp.zeros((part, width), F32), jnp.zeros((1, width), F32)), unroll=4)
 
         def back(k):
             peer = seq_peer(k)
@@ -289,8 +336,15 @@
         over(ns - 1, back, 1)
         target[q, columns(s, part), :] = result[q, s]
 
-    def states_here(q, target, sem):
-        arrived(target.at[q, 0 : (ns - 1) * part, :], sem + q)
+    def scan_back(q):
+        scan(q, r.g_in, r.g_res, r.d_bound, r.d_code, D, G, 2 * seqs, True)
+
+    def scan_on(q):
+        scan(q, r.f_in, r.f_res, r.s_bound, r.s_code, S, F, seqs, False)
+
+    def states_here(q, codes, bounds, target, sem):
+        arrived(codes.at[q, 0 : (ns - 1) * part, :], sem + q)
+        target[q] = decode(codes[q], bounds[q, s])
 
     def send_rows(q, source, target_of, sem):
         def one(k):
@@ -305,12 +359,32 @@
     own_gx = []
 
     def grad_x(q):
-        states_here(q, r.d_all, D)
+        states_here(q, r.d_code, r.d_bound, r.d_all, D)
         r.xc[q] = r.w_wide[q] * dot_split(b_of(q), r.d_all[q])
         r.xp[q] = jnp.transpose(r.z_t[q]) + r.xc[q]
         r.gx[q] = (skip_row * r.gy[q].astype(F32) + r.xp[q]).astype(BF16)
         send_rows(q, r.gx, gx_slot, GX)
-        own_gx.append(local(r.gx.at[q, columns(h, rows), :], gx_slot(q), 5 + q))
+        own_gx.append(local(r.gx.at[q, columns(h, rows), :], gx_slot(q), 4 + q))
+
+    def hand_over(q, value, slices, sem):
+        slices[q] = value.astype(BF16).reshape(chips, 2, rows, STATE)
+        remote(slices.at[q, :, 1 - core], slices.at[seqs + q, :, 0], sem + q, other)
+
+    own_group = []
+
+    def join(q, slices, sums, out, sem_in, sem, number):
+        arrived(slices.at[seqs + q, :, 0], sem_in + q)
+        sums[q] = (slices[q, :, core].astype(F32) + slices[seqs + q, :, 0].astype(F32)).astype(BF16)
+
+        def slot():
+            return out.at[q, :, columns(chip, STATE)]
+
+        def one(k):
+            peer = head_peer(k)
+            remote(sums.at[q, peer // 2], slot(), sem + q, (s, peer))
+
+        over(chips - 1, one, 2, 2)
+        own_group.append(local(sums.at[q, chip], slot(), number))
 
     def grad_b(q):
         first, second = split(jnp.transpose(r.d_scores[q]), 2)
@@ -318,27 +392,27 @@
         d_hi, d_lo = split(r.d_all[q], 2)
         value = value + dot(r.xs_hi[q], d_hi, NT)
         value = value + (dot(r.xs_hi[q], d_lo, NT) + dot(r.xs_lo[q], d_hi, NT))
-        r.gb[q] = value.astype(BF16)
-        send_rows(q, r.gb, lambda q: r.gb_all.at[q, h], GB)
-        r.gb_all[q, h] = r.gb[q, columns(h, rows), :]
-
-    own_y = []
-
-    def finish(q):
-        states_here(q, r.s_all, S)
+        hand_over(q, value, r.gb, GB2)
+
+    def join_b(q):
+        join(q, r.gb, r.gb_sum, r.gb_out, GB2, GB, 4 + seqs + q)
+
+    def join_c(q):
+        join(q, r.gc, r.gc_sum, r.gc_out, GC2, GC, 4 + 2 * seqs + q)
+
+    def grad_c(q):
+        states_here(q, r.s_code, r.s_bound, r.s_all, S)
         s_hi, s_lo = split(r.s_all[q], 2)
         first, second = split(r.d_scores[q], 2)
         value = dot(first, b_of(q)) + dot(second, b_of(q))
         value = value + dot(r.gys_hi[q], s_hi, NT)
         value = value + (dot(r.gys_hi[q], s_lo, NT) + dot(r.gys_lo[q], s_hi, NT))
-        r.gc[q] = value.astype(BF16)
-        send_rows(q, r.gc, lambda q: r.gc_all.at[q, h], GC)
-        r.gc_all[q, h] = r.gc[q, columns(h, rows), :]
-
-        y = r.y_in[q] + r.e_wide[q] * (dot(c_of(q), s_hi) + dot(c_of(q), s_lo))
+        hand_over(q, value, r.gc, GC2)
+
+    def outputs(q):
+        y = r.y_in[q] + r.e_wide[q] * dot_split(c_of(q), r.s_all[q])
         x = x_of(q).astype(F32)
-        r.y[q] = (y + skip_row * x).astype(BF16)
-        own_y.append(local(r.y.at[q], r.y_out.at[q], 5 + seqs + q))
+        r.y_out[q] = (y + skip_row * x).astype(BF16)
 
         dt = r.dt[q]
         v = times_exact(x * r.xp[q], gather)
@@ -348,53 +422,63 @@
         )
         at_last = times_exact(jnp.broadcast_to(at_last, (8, width)), gather)[:1]
         d_sum = exact_times(upper, d_cum) + at_last
-        grad = (v / dt + rate * d_sum) * jax.nn.sigmoid(r.raw[q])
-        r.gd[q] = grad.astype(BF16)
-        send_rows(q, r.gd, lambda q: r.gd_all.at[q, h], GD)
-        r.gd_all[q, h] = r.gd[q, columns(h, rows), :]
-
-    for q in range(seqs):
-        decays(q)
-    own[3].wait()
+        r.gd_wide[q] = (v / dt + rate * d_sum) * jax.nn.sigmoid(r.raw[q])
+
+    def send_steps():
+        lane = iota((STRETCH, LANES), 1)
+        packed = r.gd_wide[0]
+        for q in range(1, seqs):
+            packed = jnp.where(lane // heads == q, pltpu.roll(r.gd_wide[q], q * heads, 1), packed)
+        r.gd[...] = packed.astype(BF16)
+
+        def one(k):
+            peer = head_peer(k)
+            remote(r.gd.at[columns(peer, rows), :], r.gd_all.at[h], GD, (s, peer))
+
+        over(nh - 1, one, 1)
+        r.gd_all[h] = r.gd[columns(h, rows), :]
+
+    decays(0)
+    arrived(r.tot_all.at[0 : ns - 1], TOT)
+    r.wide[...] = times_exact(r.tot_all[...].reshape(ns * 8, LANES), spread)
+    decays(1)
+    scan_back(0)
+    scan_back(1)
+    own[2].wait()
     send_state(0)
-    arrived(r.tot_all.at[0 : ns - 1], TOT)
-    r.factor[...] = jnp.exp(times_exact(r.tot_all[...].reshape(ns * 8, LANES), spread))
-    scan(0, r.g_in, r.g_res, r.d_all, D, G, True)
     within(0)
     send_state(1)
-    scan(1, r.g_in, r.g_res, r.d_all, D, G, True)
     grad_x(0)
-    scan(0, r.f_in, r.f_res, r.s_all, S, F, False)
+    grad_x(1)
+    scan_on(0)
     within(1)
     grad_b(0)
-    grad_x(1)
-    scan(1, r.f_in, r.f_res, r.s_all, S, F, False)
+    scan_on(1)
     grad_b(1)
-    finish(0)
-    finish(1)
-
-    for q in range(seqs):
-        arrived(r.gb_all.at[q, 0 : nh - 1], GB + q)
-        for g in range(chips):
-            both = r.gb_all[q, 2 * g].astype(F32) + r.gb_all[q, 2 * g + 1].astype(F32)
-            r.gb_out[q, :, g * STATE : (g + 1) * STATE] = both.astype(BF16)
-    for q in range(seqs):
-        arrived(r.gc_all.at[q, 0 : nh - 1], GC + q)
-        for g in range(chips):
-            both = r.gc_all[q, 2 * g].astype(F32) + r.gc_all[q, 2 * g + 1].astype(F32)
-            r.gc_out[q, :, g * STATE : (g + 1) * STATE] = both.astype(BF16)
-    place_at = (LANES, all_heads)
-    for q in range(seqs):
-        arrived(r.gd_all.at[q, 0 : nh - 1], GD + q)
+    join_b(0)
+    join_b(1)
+    grad_c(0)
+    outputs(0)
+    join_c(0)
+    grad_c(1)
+    outputs(1)
+    send_steps()
+    join_c(1)
+
+    arrived(r.gd_all.at[0 : nh - 1], GD)
+    for q in range(seqs):
         total = jnp.zeros((rows, all_heads), F32)
         for p in range(nh):
-            place = one_hot((iota(place_at, 1) == p * heads + iota(place_at, 0)) & (iota(place_at, 0) < heads))
-            total = total + dot(r.gd_all[q, p], place)
+            moved = pltpu.roll(r.gd_all[p].astype(F32), (p - q) * heads % LANES, 1)[:, :all_heads]
+            total = jnp.where(pack_lane // heads == p, moved, total)
         r.gdt_out[q] = total.astype(BF16)
     for q in range(seqs):
         arrived(r.gx_out.at[q, :, 0 : (nh - 1) * width], GX + q)
-
-    left(r.dt_all.at[:, 0 : nh - 1], DT)
+        arrived(r.gb_out.at[q, :, 0 : (chips - 1) * STATE], GB + q)
+        arrived(r.gc_out.at[q, :, 0 : (chips - 1) * STATE], GC + q)
+
+    left(r.dt_all.at[0 : nh - 1], DT)
+    left(r.gd_all.at[0 : nh - 1], GD)
     left(r.c_all.at[:, 0 : chips - 1, 0], C)
     left(r.c_all.at[:, :, 0], C2)
     left(r.b_all.at[:, 0 : chips - 1, 0], B)
@@ -407,10 +491,20 @@
         left(r.f_in.at[q, 0 : ns - 1], F + q)
         left(r.f_res.at[q, 0 : ns - 1], S + q)
         left(r.gx.at[q, 0 : (nh - 1) * rows, :], GX + q)
-        left(r.gb_all.at[q, 0 : nh - 1], GB + q)
-        left(r.gc_all.at[q, 0 : nh - 1], GC + q)
-        left(r.gd_all.at[q, 0 : nh - 1], GD + q)
-    for copy in own_gx + own_y:
+        left(r.gb.at[q, :, 0], GB2 + q)
+        left(r.gc.at[q, :, 0], GC2 + q)
+        left(r.gb_sum.at[q, 0 : chips - 1], GB + q)
+        left(r.gc_sum.at[q, 0 : chips - 1], GC + q)
+    for copy in own_gx + own_group:
+        copy.wait()
+
+
+def deliver(*refs):
+    count = len(refs) // 2
+    copies = [pltpu.make_async_copy(refs[i], refs[count + i], refs[-1].at[i]) for i in range(count)]
+    for copy in copies:
+        copy.start()
+    for copy in copies:
         copy.wait()
 
 
@@ -422,7 +516,8 @@
     part = STATE // ns
     chips = nh // 2
     scratch = {
-        "dt_all": ((seqs, nh, rows, all_heads), BF16),
+        "dt_pack": ((nh, rows, all_heads), BF16),
+        "dt_all": ((nh, rows, all_heads), BF16),
         "c_all": ((seqs, chips, 2, rows, STATE), BF16),
         "b_all": ((seqs, chips, 2, rows, STATE), BF16),
         "x_all": ((seqs, nh, rows, width), BF16),
@@ -432,7 +527,8 @@
         "dt": ((seqs, STRETCH, LANES), F32),
         "tot_send": ((8, LANES), F32),
         "tot_all": ((ns, 8, LANES), F32),
-        "factor": ((ns * 8, width), F32),
+        "wide": ((ns * 8, width), F32),
+        "own_wide": ((8, width), F32),
         "w_wide": ((seqs, STRETCH, width), F32),
         "e_wide": ((seqs, STRETCH, width), F32),
         "u_row": ((seqs, heads, STRETCH), F32),
@@ -450,22 +546,24 @@
         "xc": ((seqs, STRETCH, width), F32),
         "xp": ((seqs, STRETCH, width), F32),
         "y_in": ((seqs, STRETCH, width), F32),
-        "y": ((seqs, STRETCH, width), BF16),
         "gx": ((seqs, STRETCH, width), BF16),
-        "gb": ((seqs, STRETCH, STATE), BF16),
-        "gc": ((seqs, STRETCH, STATE), BF16),
-        "gd": ((seqs, STRETCH, LANES), BF16),
-        "gb_all": ((seqs, nh, rows, STATE), BF16),
-        "gc_all": ((seqs, nh, rows, STATE), BF16),
-        "gd_all": ((seqs, nh, rows, LANES), BF16),
+        "gb": ((2 * seqs, chips, 2, rows, STATE), BF16),
+        "gc": ((2 * seqs, chips, 2, rows, STATE), BF16),
+        "gb_sum": ((seqs, chips, rows, STATE), BF16),
+        "gc_sum": ((seqs, chips, rows, STATE), BF16),
+        "gd_wide": ((seqs, STRETCH, LANES), F32),
+        "gd": ((STRETCH, LANES), BF16),
+        "gd_all": ((nh, rows, LANES), BF16),
     }
     for name in ("g", "f"):
-        scratch[name + "_out"] = ((seqs, STATE, width), F32)
-        scratch[name + "_in"] = ((seqs, ns, part, width), F32)
-        scratch[name + "_res"] = ((seqs, ns, part, width), F32)
-    for name in ("d_all", "s_all"):
-        scratch[name] = ((seqs, STATE, width), F32)
-    sems = 6 + 9 * seqs
+        scratch[name + "_out"] = ((seqs, STATE, width), BF16)
+        scratch[name + "_in"] = ((seqs, ns, part, width), BF16)
+        scratch[name + "_res"] = ((seqs, ns, part, width), BF16)
+    for name in ("d", "s"):
+        scratch[name + "_all"] = ((seqs, STATE, width), F32)
+        scratch[name + "_code"] = ((seqs, STATE, width), BF16)
+        scratch[name + "_bound"] = ((seqs, ns, 1, width), F32)
+    sems = 7 + 10 * seqs
     names = (
         ["a_log", "skip", "x_in", "b_in", "c_in", "dt_in", "gy_in"]
         + ["y_out", "gx_out", "gb_out", "gc_out", "gdt_out"]
@@ -484,22 +582,31 @@
     def like(array):
         return jax.ShapeDtypeStruct(array.shape, BF16)
 
-    return pl.pallas_call(
+    results = pl.pallas_call(
         body,
-        out_shape=(like(grad_y), like(x_in), like(b_in), like(c_in), like(dt_in)),
-        in_specs=[small, small] + [anywhere] * 5,
-        out_specs=(anywhere, anywhere, vmem, vmem, vmem),
+        out_shape=tuple(pltpu.VMEM(array.shape, BF16) for array in (grad_y, x_in, b_in, c_in, dt_in)),
+        in_specs=[small, small, anywhere, anywhere, anywhere, vmem, anywhere],
+        out_specs=(vmem,) * 5,
         scratch_shapes=[pltpu.VMEM(shape, dtype) for shape, dtype in scratch.values()]
         + [
             pltpu.SemaphoreType.DMA((sems,)),
             pltpu.SemaphoreType.DMA((sems,)),
-            pltpu.SemaphoreType.DMA((5 + 2 * seqs,)),
+            pltpu.SemaphoreType.DMA((4 + 3 * seqs,)),
         ],
         compiler_params=pltpu.CompilerParams(
             collective_id=0, has_side_effects=True, vmem_limit_bytes=56 * 1024 * 1024
         ),
         name="mixer",
     )(a_log, skip_gain, x_in, b_in, c_in, dt_in, grad_y)
+    results = [pltpu.with_memory_space_constraint(result, pltpu.VMEM) for result in results]
+    return pl.pallas_call(
+        deliver,
+        out_shape=tuple(like(result) for result in results),
+        in_specs=[anywhere] * len(results),
+        out_specs=(anywhere,) * len(results),
+        scratch_shapes=[pltpu.SemaphoreType.DMA((len(results),))],
+        name="deliver",
+    )(*results)
 
 
 def solution(mesh):

time: 87.5 us -> 61 us (0.70)
  Pallas kernels: 81.5 us -> 60.2 us
  local copies, waits for them, and re-layouts: 5.2 us -> 0 us
    pallas_call x1 -> x2, Pallas kernels: 81.5 us -> 60.2 us  [the longest x1 59.1 us: on_device(): pl.pallas_call(body, out_shape=tuple((pltpu.VMEM(array.shape, BF16) for a...]
    unnamed x13 -> x0, local copies, waits for them, and re-layouts: 5.2 us -> none
where the time goes in v2:
time: 61 us; the launch traced here: 60.8 us
  Pallas kernels  60.2 us (99%)
  between operations  0.64 us (1%)
    pallas_call x1, Pallas kernels, on_device(): pl.pallas_call(body, out_shape=tuple((pltpu.VMEM(array.shape, BF16) for a...  59.1 us

profile of v2, /device:TPU:1, one launch (start us, length us, event | category | flops | bytes accessed | tf_op | source)
XLA Modules:
  0.0 60.8 jit_solution(7929620870662765058)
XLA Ops:
  0.6 59.1 %mixer.1 = (bf16[2,256,512]{2,1,0:T(8,128)(2,1)S(1)}, bf16[2,16,8192]{2,1,0:T(8,128)(2,1)S(1)}, bf16[2,16,2048]{2,1,0:T(8,128)(2,1)S(1)}, bf16[2,16,2048]{2,1,0:T(8,128)(2,1)S(1)}, bf16[2,16,128]{2,1,0:T(8,128)(2,1)S(1)}) custom-call(f32[8]{0:T(128)} %refs_0_.1, f32[8]{0:T(128)} %refs_1_.1, bf16[2,16,8192]{2,1,0:T(8,128)(2,1)} %refs_2_.1, ...), custom_call_target="tpu_custom_call" | custom-call | tf_op jit(solution)/shard_map/mixer/pallas_call | solution.py:585
  59.7 1.1 %deliver.1 = (bf16[2,256,512]{2,1,0:T(8,128)(2,1)}, bf16[2,16,8192]{2,1,0:T(8,128)(2,1)}, bf16[2,16,2048]{2,1,0:T(8,128)(2,1)}, bf16[2,16,2048]{2,1,0:T(8,128)(2,1)}, bf16[2,16,128]{2,1,0:T(8,128)(2,1)}) custom-call(bf16[2,256,512]{2,1,0:T(8,128)(2,1)S(1)} %get-tuple-element.10.refs_0_, bf16[2,16,8192]{2,1,0:T(8,128)(2,1)S(1)} %get-tuple-element.11.refs_1_, ...), custom_call_target="tpu_custom_call" | custom-call | tf_op jit(solution)/shard_map/deliver/pallas_call | solution.py:602

commit v3 on v2

--- a/solution.py
+++ b/solution.py
@@ -93,11 +93,17 @@
     chip = h // 2
     other = (s, h + 1 - 2 * core)
 
-    def head_peer(k):
-        return lax.rem(h + k, nh)
-
-    def seq_peer(k):
-        return lax.rem(s + k, ns)
+    def out_and_in(i, count):
+        return count // 2 + (2 * (i % 2) - 1) * ((i + 1) // 2)
+
+    def head_peer(i):
+        return lax.rem(h + out_and_in(i, nh), nh)
+
+    def same_core_peer(i):
+        return lax.rem(h + 2 * out_and_in(i, chips), nh)
+
+    def seq_peer(i):
+        return lax.rem(s + 1 + i, ns)
 
     def remote(src, dst, sem, device):
         pltpu.make_async_remote_copy(
@@ -115,9 +121,9 @@
     def left(ref, sem):
         pltpu.make_async_copy(ref, ref, r.send_sem.at[sem]).wait()
 
-    def over(count, body, start=0, step=1):
+    def over(count, body):
         def one(i, carry):
-            body(start + i * step)
+            body(i)
             return carry
 
         lax.fori_loop(0, count, one, 0)
@@ -136,8 +142,8 @@
     def greet_seq(k):
         pl.semaphore_signal(barrier, inc=1, device_id=(seq_peer(k), h), device_id_type=MESH)
 
-    over(nh - 1, greet_head, 1)
-    over(ns - 1, greet_seq, 1)
+    over(nh - 1, greet_head)
+    over(ns - 1, greet_seq)
 
     own = [
         local(r.c_in.at[:, :, columns(chip, STATE)], r.c_all.at[:, chip, core], 0),
@@ -146,15 +152,27 @@
         local(r.gy_in, r.gy, 3),
     ]
 
-    all_heads = r.dt_in.shape[2]
-    pack_lane = iota((rows, all_heads), 1)
-    raw_dt = [r.dt_in[q].astype(F32) for q in range(seqs)]
-    for p in range(nh):
-        packed = jnp.zeros((rows, all_heads), F32)
-        for q in range(seqs):
-            moved = pltpu.roll(raw_dt[q], (q - p) * heads % all_heads, 1)
-            packed = jnp.where(pack_lane // heads == q, moved, packed)
-        r.dt_pack[p] = packed.astype(BF16)
+    lane_at = iota((nh, LANES), 1)
+    group_at = lane_at // heads == iota((nh, LANES), 0)
+    regroup_at = (nh * LANES, LANES)
+    r.regroup[...] = one_hot(
+        (iota(regroup_at, 1) // heads == iota(regroup_at, 0) // LANES)
+        & (iota(regroup_at, 1) % heads == iota(regroup_at, 0) % heads)
+    )
+
+    def regrouped(row_of):
+        return dot(
+            jnp.concatenate(
+                [jnp.where(group_at, row_of(i), 0.0).astype(BF16) for i in range(nh)], axis=1
+            ),
+            r.regroup[...],
+        )
+
+    for q in range(seqs):
+        raw = r.dt_in[q].astype(F32)
+        packed = regrouped(lambda i, raw=raw: raw[i : i + 1, :])
+        for p in range(nh):
+            r.dt_pack[p, :, q * LANES : (q + 1) * LANES] = packed[p : p + 1, :]
     r.dt_all[h] = r.dt_pack[h]
     own[3].wait()
     for q in range(seqs):
@@ -167,23 +185,23 @@
         remote(r.dt_pack.at[peer], r.dt_all.at[h], DT, (s, peer))
 
     def send_c(k):
-        peer = head_peer(k)
+        peer = same_core_peer(k)
         remote(r.c_in.at[:, :, columns(peer // 2, STATE)], r.c_all.at[:, chip, core], C, (s, peer))
 
     def send_b(k):
-        peer = head_peer(k)
+        peer = same_core_peer(k)
         remote(r.b_in.at[:, :, columns(peer // 2, STATE)], r.b_all.at[:, chip, core], B, (s, peer))
 
-    over(nh - 1, send_dt, 1)
-    over(chips - 1, send_c, 2, 2)
-    over(chips - 1, send_b, 2, 2)
+    over(nh - 1, send_dt)
+    over(chips - 1, send_c)
+    over(chips - 1, send_b)
     for q in range(seqs):
 
         def send_x(k, q=q):
             peer = head_peer(k)
             remote(r.x_in.at[q, :, columns(peer, width)], r.x_all.at[q, h], X + q, (s, peer))
 
-        over(nh - 1, send_x, 1)
+        over(nh - 1, send_x)
 
     lane_row = iota((1, LANES), 1)
     rate = jnp.zeros((1, LANES), F32)
@@ -200,10 +218,19 @@
     upper = one_hot(iota((STRETCH, STRETCH), 0) <= iota((STRETCH, STRETCH), 1))
 
     arrived(r.dt_all.at[0 : nh - 1], DT)
-    raw_all = r.dt_all[...].reshape(STRETCH, all_heads).astype(F32)
+    token_lane = iota((STRETCH, LANES), 1) // heads == iota((STRETCH, LANES), 0) % rows
+    head_of_lane = iota((LANES, LANES), 0) % heads == iota((LANES, LANES), 1)
+    lane_of_head = iota((LANES, LANES), 1) % heads == iota((LANES, LANES), 0)
     r.tot_send[...] = jnp.zeros_like(r.tot_send)
     for q in range(seqs):
-        raw = raw_all if q == 0 else pltpu.roll(raw_all, all_heads - q * heads, 1)
+        by_device = jnp.concatenate(
+            [
+                jnp.broadcast_to(r.dt_all[p, :, q * LANES : (q + 1) * LANES], (rows, LANES))
+                for p in range(nh)
+            ],
+            axis=0,
+        )
+        raw = dot(jnp.where(token_lane, by_device, 0.0).astype(BF16), one_hot(head_of_lane))
         dt = jnp.maximum(raw, 0.0) + jnp.log1p(jnp.exp(-jnp.abs(raw)))
         cum = exact_times(lower, dt * rate)
         last = cum[STRETCH - 1 :, :]
@@ -214,16 +241,14 @@
         r.tot_send[pl.ds(q, 1), :] = last
         r.tot_send[pl.ds(seqs + q, 1), :] = X_B * jnp.sum(weight, axis=0, keepdims=True)
         r.tot_send[pl.ds(2 * seqs + q, 1), :] = GY_C * jnp.sum(growth, axis=0, keepdims=True)
-        r.w_wide[q] = times_exact(weight, spread)
+        r.weight[q] = weight
+        r.cum[q] = cum
         r.e_wide[q] = times_exact(growth, spread)
-        r.u_row[q] = jnp.transpose(cum - jnp.log(dt))[:heads, :]
-        for e in range(heads):
-            r.cum_col[q, e] = jnp.broadcast_to(cum[:, e : e + 1], (STRETCH, LANES))
 
     def send_tot(k):
         remote(r.tot_send, r.tot_all.at[s], TOT, (seq_peer(k), h))
 
-    over(ns - 1, send_tot, 1)
+    over(ns - 1, send_tot)
     r.tot_all[s] = r.tot_send[...]
     r.own_wide[...] = times_exact(r.tot_send[...], spread)
 
@@ -237,9 +262,6 @@
         first, second = split(r.gy[q].astype(F32) * r.e_wide[q], 2)
         r.gys_hi[q] = first
         r.gys_lo[q] = second
-    own[1].wait()
-    arrived(r.b_all.at[:, 0 : chips - 1, 0], B)
-    remote(r.b_all.at[:, :, core], r.b_all.at[:, :, core], B2, other)
     arrived(r.c_all.at[:, :, 0], C2)
 
     def c_of(q):
@@ -256,7 +278,7 @@
             peer = seq_peer(k)
             remote(source.at[q, columns(peer, part), :], target.at[q, s], sem + q, (peer, h))
 
-        over(ns - 1, one, 1)
+        over(ns - 1, one)
         target[q, s] = source[q, columns(s, part), :]
 
     for q in range(seqs):
@@ -264,6 +286,16 @@
         r.g_out[q] = encode(state, own_bound(2 * seqs + q))
         send_parts(q, r.g_out, r.g_in, G)
 
+    for q in range(seqs):
+        cum = r.cum[q]
+        r.w_wide[q] = times_exact(r.weight[q], spread)
+        r.u_row[q] = jnp.transpose(cum - jnp.log(r.dt[q]))[:heads, :]
+        for e in range(heads):
+            r.cum_col[q, e] = jnp.broadcast_to(cum[:, e : e + 1], (STRETCH, LANES))
+
+    own[1].wait()
+    arrived(r.b_all.at[:, 0 : chips - 1, 0], B)
+    remote(r.b_all.at[:, :, core], r.b_all.at[:, :, core], B2, other)
     arrived(r.b_all.at[:, :, 0], B2)
 
     def decays(q):
@@ -333,7 +365,7 @@
             peer = seq_peer(k)
             remote(result.at[q, peer], target.at[q, columns(s, part), :], sem + q, (peer, h))
 
-        over(ns - 1, back, 1)
+        over(ns - 1, back)
         target[q, columns(s, part), :] = result[q, s]
 
     def scan_back(q):
@@ -351,7 +383,7 @@
             peer = head_peer(k)
             remote(source.at[q, columns(peer, rows), :], target_of(q), sem + q, (s, peer))
 
-        over(nh - 1, one, 1)
+        over(nh - 1, one)
 
     def gx_slot(q):
         return r.gx_out.at[q, :, columns(h, width)]
@@ -380,10 +412,10 @@
             return out.at[q, :, columns(chip, STATE)]
 
         def one(k):
-            peer = head_peer(k)
+            peer = same_core_peer(k)
             remote(sums.at[q, peer // 2], slot(), sem + q, (s, peer))
 
-        over(chips - 1, one, 2, 2)
+        over(chips - 1, one)
         own_group.append(local(sums.at[q, chip], slot(), number))
 
     def grad_b(q):
@@ -425,35 +457,35 @@
         r.gd_wide[q] = (v / dt + rate * d_sum) * jax.nn.sigmoid(r.raw[q])
 
     def send_steps():
-        lane = iota((STRETCH, LANES), 1)
-        packed = r.gd_wide[0]
-        for q in range(1, seqs):
-            packed = jnp.where(lane // heads == q, pltpu.roll(r.gd_wide[q], q * heads, 1), packed)
-        r.gd[...] = packed.astype(BF16)
+        for q in range(seqs):
+            values = dot(r.gd_wide[q].astype(BF16), one_hot(lane_of_head))
+            values = jnp.where(token_lane, values, 0.0).reshape(nh, rows, LANES).sum(axis=1)
+            for p in range(nh):
+                r.gd_pack[p, :, q * LANES : (q + 1) * LANES] = values[p : p + 1, :]
 
         def one(k):
             peer = head_peer(k)
-            remote(r.gd.at[columns(peer, rows), :], r.gd_all.at[h], GD, (s, peer))
-
-        over(nh - 1, one, 1)
-        r.gd_all[h] = r.gd[columns(h, rows), :]
+            remote(r.gd_pack.at[peer], r.gd_all.at[h], GD, (s, peer))
+
+        over(nh - 1, one)
+        r.gd_all[h] = r.gd_pack[h]
 
     decays(0)
     arrived(r.tot_all.at[0 : ns - 1], TOT)
     r.wide[...] = times_exact(r.tot_all[...].reshape(ns * 8, LANES), spread)
-    decays(1)
     scan_back(0)
     scan_back(1)
     own[2].wait()
     send_state(0)
-    within(0)
+    decays(1)
     send_state(1)
     grad_x(0)
     grad_x(1)
+    within(0)
     scan_on(0)
     within(1)
+    scan_on(1)
     grad_b(0)
-    scan_on(1)
     grad_b(1)
     join_b(0)
     join_b(1)
@@ -467,11 +499,7 @@
 
     arrived(r.gd_all.at[0 : nh - 1], GD)
     for q in range(seqs):
-        total = jnp.zeros((rows, all_heads), F32)
-        for p in range(nh):
-            moved = pltpu.roll(r.gd_all[p].astype(F32), (p - q) * heads % LANES, 1)[:, :all_heads]
-            total = jnp.where(pack_lane // heads == p, moved, total)
-        r.gdt_out[q] = total.astype(BF16)
+        r.gdt_out[q] = regrouped(lambda i, q=q: r.gd_all[i, :, q * LANES : (q + 1) * LANES]).astype(BF16)
     for q in range(seqs):
         arrived(r.gx_out.at[q, :, 0 : (nh - 1) * width], GX + q)
         arrived(r.gb_out.at[q, :, 0 : (chips - 1) * STATE], GB + q)
@@ -516,8 +544,9 @@
     part = STATE // ns
     chips = nh // 2
     scratch = {
-        "dt_pack": ((nh, rows, all_heads), BF16),
-        "dt_all": ((nh, rows, all_heads), BF16),
+        "regroup": ((nh * LANES, LANES), BF16),
+        "dt_pack": ((nh, 1, seqs * LANES), F32),
+        "dt_all": ((nh, 1, seqs * LANES), F32),
         "c_all": ((seqs, chips, 2, rows, STATE), BF16),
         "b_all": ((seqs, chips, 2, rows, STATE), BF16),
         "x_all": ((seqs, nh, rows, width), BF16),
@@ -525,6 +554,8 @@
         "gy_t": ((seqs, width, STRETCH), BF16),
         "raw": ((seqs, STRETCH, LANES), F32),
         "dt": ((seqs, STRETCH, LANES), F32),
+        "weight": ((seqs, STRETCH, LANES), F32),
+        "cum": ((seqs, STRETCH, LANES), F32),
         "tot_send": ((8, LANES), F32),
         "tot_all": ((ns, 8, LANES), F32),
         "wide": ((ns * 8, width), F32),
@@ -552,8 +583,8 @@
         "gb_sum": ((seqs, chips, rows, STATE), BF16),
         "gc_sum": ((seqs, chips, rows, STATE), BF16),
         "gd_wide": ((seqs, STRETCH, LANES), F32),
-        "gd": ((STRETCH, LANES), BF16),
-        "gd_all": ((nh, rows, LANES), BF16),
+        "gd_pack": ((nh, 1, seqs * LANES), F32),
+        "gd_all": ((nh, 1, seqs * LANES), F32),
     }
     for name in ("g", "f"):
         scratch[name + "_out"] = ((seqs, STATE, width), BF16)

time: 61 us -> 57.6 us (0.944)
  Pallas kernels: 60.2 us -> 56.8 us
    pallas_call x1, Pallas kernels: 59.1 us -> 55.7 us  [on_device(): pl.pallas_call(body, out_shape=tuple((pltpu.VMEM(array.shape, BF16) for a...]
where the time goes in v3:
time: 57.6 us; the launch traced here: 57.4 us
  Pallas kernels  56.8 us (99%)
  between operations  0.64 us (1%)
    pallas_call x1, Pallas kernels, on_device(): pl.pallas_call(body, out_shape=tuple((pltpu.VMEM(array.shape, BF16) for a...  55.7 us

profile of v3, /device:TPU:1, one launch (start us, length us, event | category | flops | bytes accessed | tf_op | source)
XLA Modules:
  0.0 57.4 jit_solution(8978590799539206813)
XLA Ops:
  0.6 55.7 %mixer.1 = (bf16[2,256,512]{2,1,0:T(8,128)(2,1)S(1)}, bf16[2,16,8192]{2,1,0:T(8,128)(2,1)S(1)}, bf16[2,16,2048]{2,1,0:T(8,128)(2,1)S(1)}, bf16[2,16,2048]{2,1,0:T(8,128)(2,1)S(1)}, bf16[2,16,128]{2,1,0:T(8,128)(2,1)S(1)}) custom-call(f32[8]{0:T(128)} %refs_0_.1, f32[8]{0:T(128)} %refs_1_.1, bf16[2,16,8192]{2,1,0:T(8,128)(2,1)} %refs_2_.1, ...), custom_call_target="tpu_custom_call" | custom-call | tf_op jit(solution)/shard_map/mixer/pallas_call | solution.py:616
  56.4 1.1 %deliver.1 = (bf16[2,256,512]{2,1,0:T(8,128)(2,1)}, bf16[2,16,8192]{2,1,0:T(8,128)(2,1)}, bf16[2,16,2048]{2,1,0:T(8,128)(2,1)}, bf16[2,16,2048]{2,1,0:T(8,128)(2,1)}, bf16[2,16,128]{2,1,0:T(8,128)(2,1)}) custom-call(bf16[2,256,512]{2,1,0:T(8,128)(2,1)S(1)} %get-tuple-element.10.refs_0_, bf16[2,16,8192]{2,1,0:T(8,128)(2,1)S(1)} %get-tuple-element.11.refs_1_, ...), custom_call_target="tpu_custom_call" | custom-call | tf_op jit(solution)/shard_map/deliver/pallas_call | solution.py:633

commit v4 on v3

--- a/solution.py
+++ b/solution.py
@@ -10,6 +10,7 @@
 HEAD_DIM = 64
 STATE = 256
 STRETCH = 256
+CUTS = 1
 LANES = 128
 MESH = pl.DeviceIdType.MESH
 F32 = jnp.float32
@@ -59,7 +60,7 @@
 
 
 def encode(value, bound):
-    share = jnp.maximum(jnp.abs(value) / jnp.maximum(bound, TINY), TINY)
+    share = jnp.maximum(jnp.abs(value) * (1.0 / jnp.maximum(bound, TINY)), TINY)
     level = jnp.exp2(jnp.log(share) * (0.125 / LN2))
     code = jnp.exp2(level * CODE_SPAN - 0.5 * CODE_SPAN)
     return jnp.where(value < 0.0, -code, code).astype(BF16)
@@ -88,6 +89,7 @@
     width = heads * HEAD_DIM
     part = STATE // ns
     chips = nh // 2
+    half = width // CUTS
     s, h = lax.axis_index("seq"), lax.axis_index("head")
     core = lax.rem(h, 2)
     chip = h // 2
@@ -132,7 +134,8 @@
         return pl.ds(pl.multiple_of(index * size, size), size)
 
     DT, C, C2, B, B2, TOT, GD = range(7)
-    X, G, D, F, S, GX, GB, GC, GB2, GC2 = (7 + seqs * i for i in range(10))
+    X, F, S, GX, GB, GC, GB2, GC2 = (7 + seqs * i for i in range(8))
+    G, D = (7 + seqs * (8 + CUTS * i) for i in range(2))
 
     barrier = pltpu.get_barrier_semaphore()
 
@@ -273,18 +276,23 @@
     def x_of(q):
         return r.x_all[q].reshape(STRETCH, width)
 
-    def send_parts(q, source, target, sem):
+    def piece(c):
+        return pl.ds(c * half, half)
+
+    def send_parts(q, source, target, sem, cols):
         def one(k):
             peer = seq_peer(k)
-            remote(source.at[q, columns(peer, part), :], target.at[q, s], sem + q, (peer, h))
+            remote(source.at[q, columns(peer, part), cols], target.at[q, s, :, cols], sem, (peer, h))
 
         over(ns - 1, one)
-        target[q, s] = source[q, columns(s, part), :]
-
-    for q in range(seqs):
-        state = dot(c_of(q), r.gys_hi[q], TN) + dot(c_of(q), r.gys_lo[q], TN)
-        r.g_out[q] = encode(state, own_bound(2 * seqs + q))
-        send_parts(q, r.g_out, r.g_in, G)
+        target[q, s, :, cols] = source[q, columns(s, part), cols]
+
+    for q in range(seqs):
+        for c in range(CUTS):
+            cols = piece(c)
+            state = dot(c_of(q), r.gys_hi[q, :, cols], TN) + dot(c_of(q), r.gys_lo[q, :, cols], TN)
+            r.g_out[q, :, cols] = encode(state, r.own_wide[pl.ds(2 * seqs + q, 1), cols])
+            send_parts(q, r.g_out, r.g_in, G + q * CUTS + c, cols)
 
     for q in range(seqs):
         cum = r.cum[q]
@@ -298,10 +306,12 @@
     remote(r.b_all.at[:, :, core], r.b_all.at[:, :, core], B2, other)
     arrived(r.b_all.at[:, :, 0], B2)
 
-    def decays(q):
-        r.scores[q] = dot(c_of(q), b_of(q), NT)
-
-        def one(e):
+    def decays(q, c):
+        if c == 0:
+            r.scores[q] = dot(c_of(q), b_of(q), NT)
+
+        def one(i):
+            e = c * (heads // CUTS) + i
             column = r.cum_col[q, e]
             gap = jnp.concatenate([column, column], axis=1) - r.u_row[q, pl.ds(e, 1), :]
             decay = jnp.where(causal, jnp.exp(gap), 0.0)
@@ -313,7 +323,7 @@
             grad = r.gy_t[q, rows_e, :]
             r.z_t[q, rows_e, :] = dot(grad, first) + dot(grad, second)
 
-        over(heads, one)
+        over(heads // CUTS, one)
 
     def send_state(q):
         arrived(r.x_all.at[q, 0 : nh - 1], X + q)
@@ -322,7 +332,7 @@
         r.xs_lo[q] = second
         state = dot(b_of(q), first, TN) + dot(b_of(q), second, TN)
         r.f_out[q] = encode(state, own_bound(seqs + q))
-        send_parts(q, r.f_out, r.f_in, F)
+        send_parts(q, r.f_out, r.f_in, F + q, pl.ds(0, width))
 
     def within(q):
         r.d_scores[q] = jnp.zeros((STRETCH, STRETCH), F32)
@@ -344,59 +354,66 @@
 
         over(heads // 2, one)
 
-    def scan(q, source, result, bounds, target, sem, sem_in, bound_row, reverse):
-        arrived(source.at[q, 0 : ns - 1], sem_in + q)
+    def scan(q, source, result, bounds, target, sem, sem_in, bound_row, reverse, cols):
+        arrived(source.at[q, 0 : ns - 1, :, cols], sem_in)
 
         def wide(block, row):
-            return r.wide[pl.ds(block * 8 + row, 1), :]
+            return r.wide[pl.ds(block * 8 + row, 1), cols]
 
         def one(i, carry):
             block = ns - 1 - i if reverse else i
             state, bound = carry
-            bounds[q, block] = bound
-            result[q, block] = encode(state, bound)
+            bounds[q, block, :, cols] = bound
+            result[q, block, :, cols] = encode(state, bound)
             factor = jnp.exp(wide(block, q))
             block_bound = wide(block, bound_row + q)
-            return (factor * state + decode(source[q, block], block_bound), factor * bound + block_bound)
-
-        lax.fori_loop(0, ns, one, (jnp.zeros((part, width), F32), jnp.zeros((1, width), F32)), unroll=4)
+            return (
+                factor * state + decode(source[q, block, :, cols], block_bound),
+                factor * bound + block_bound,
+            )
+
+        start = (jnp.zeros((part, cols.size), F32), jnp.zeros((1, cols.size), F32))
+        lax.fori_loop(0, ns, one, start, unroll=8)
 
         def back(k):
             peer = seq_peer(k)
-            remote(result.at[q, peer], target.at[q, columns(s, part), :], sem + q, (peer, h))
+            remote(
+                result.at[q, peer, :, cols], target.at[q, columns(s, part), cols], sem, (peer, h)
+            )
 
         over(ns - 1, back)
-        target[q, columns(s, part), :] = result[q, s]
-
-    def scan_back(q):
-        scan(q, r.g_in, r.g_res, r.d_bound, r.d_code, D, G, 2 * seqs, True)
+        target[q, columns(s, part), cols] = result[q, s, :, cols]
+
+    def scan_back(q, c):
+        number = q * CUTS + c
+        scan(q, r.g_in, r.g_res, r.d_bound, r.d_code, D + number, G + number, 2 * seqs, True, piece(c))
 
     def scan_on(q):
-        scan(q, r.f_in, r.f_res, r.s_bound, r.s_code, S, F, seqs, False)
-
-    def states_here(q, codes, bounds, target, sem):
-        arrived(codes.at[q, 0 : (ns - 1) * part, :], sem + q)
-        target[q] = decode(codes[q], bounds[q, s])
-
-    def send_rows(q, source, target_of, sem):
+        scan(q, r.f_in, r.f_res, r.s_bound, r.s_code, S + q, F + q, seqs, False, pl.ds(0, width))
+
+    def states_here(q, codes, bounds, target, sem, cols):
+        arrived(codes.at[q, 0 : (ns - 1) * part, cols], sem)
+        target[q, :, cols] = decode(codes[q, :, cols], bounds[q, s, :, cols])
+
+    own_gx = []
+
+    def grad_x(q, c):
+        cols = piece(c)
+        states_here(q, r.d_code, r.d_bound, r.d_all, D + q * CUTS + c, cols)
+        xc = r.w_wide[q, :, cols] * dot_split(b_of(q), r.d_all[q, :, cols])
+        xp = jnp.transpose(r.z_t[q, cols, :]) + xc
+        r.xc[q, :, cols] = xc
+        r.xp[q, :, cols] = xp
+        skip = skip_row[:, c * half : (c + 1) * half]
+        r.gx[q, :, cols] = (skip * r.gy[q, :, cols].astype(F32) + xp).astype(BF16)
+        slot = r.gx_out.at[q, :, columns(h * CUTS + c, half)]
+
         def one(k):
             peer = head_peer(k)
-            remote(source.at[q, columns(peer, rows), :], target_of(q), sem + q, (s, peer))
+            remote(r.gx.at[q, columns(peer, rows), cols], slot, GX + q, (s, peer))
 
         over(nh - 1, one)
-
-    def gx_slot(q):
-        return r.gx_out.at[q, :, columns(h, width)]
-
-    own_gx = []
-
-    def grad_x(q):
-        states_here(q, r.d_code, r.d_bound, r.d_all, D)
-        r.xc[q] = r.w_wide[q] * dot_split(b_of(q), r.d_all[q])
-        r.xp[q] = jnp.transpose(r.z_t[q]) + r.xc[q]
-        r.gx[q] = (skip_row * r.gy[q].astype(F32) + r.xp[q]).astype(BF16)
-        send_rows(q, r.gx, gx_slot, GX)
-        own_gx.append(local(r.gx.at[q, columns(h, rows), :], gx_slot(q), 4 + q))
+        own_gx.append(local(r.gx.at[q, columns(h, rows), cols], slot, 4 + q * CUTS + c))
 
     def hand_over(q, value, slices, sem):
         slices[q] = value.astype(BF16).reshape(chips, 2, rows, STATE)
@@ -427,34 +444,37 @@
         hand_over(q, value, r.gb, GB2)
 
     def join_b(q):
-        join(q, r.gb, r.gb_sum, r.gb_out, GB2, GB, 4 + seqs + q)
+        join(q, r.gb, r.gb_sum, r.gb_out, GB2, GB, 4 + CUTS * seqs + q)
 
     def join_c(q):
-        join(q, r.gc, r.gc_sum, r.gc_out, GC2, GC, 4 + 2 * seqs + q)
+        join(q, r.gc, r.gc_sum, r.gc_out, GC2, GC, 4 + (CUTS + 1) * seqs + q)
 
     def grad_c(q):
-        states_here(q, r.s_code, r.s_bound, r.s_all, S)
+        states_here(q, r.s_code, r.s_bound, r.s_all, S + q, pl.ds(0, width))
         s_hi, s_lo = split(r.s_all[q], 2)
-        first, second = split(r.d_scores[q], 2)
-        value = dot(first, b_of(q)) + dot(second, b_of(q))
-        value = value + dot(r.gys_hi[q], s_hi, NT)
+        value = r.gc_in[q] + dot(r.gys_hi[q], s_hi, NT)
         value = value + (dot(r.gys_hi[q], s_lo, NT) + dot(r.gys_lo[q], s_hi, NT))
         hand_over(q, value, r.gc, GC2)
 
+    def before_state(q):
+        x = x_of(q).astype(F32)
+        r.v[q] = times_exact(x * r.xp[q], gather)
+        r.at_last[q] = jnp.sum(x * r.xc[q], axis=0, keepdims=True)
+        first, second = split(r.d_scores[q], 2)
+        r.gc_in[q] = dot(first, b_of(q)) + dot(second, b_of(q))
+
     def outputs(q):
         y = r.y_in[q] + r.e_wide[q] * dot_split(c_of(q), r.s_all[q])
-        x = x_of(q).astype(F32)
-        r.y_out[q] = (y + skip_row * x).astype(BF16)
-
         dt = r.dt[q]
-        v = times_exact(x * r.xp[q], gather)
+        v = r.v[q]
         d_cum = times_exact(r.gy[q].astype(F32) * y, gather) - v
-        at_last = jnp.sum(x * r.xc[q], axis=0, keepdims=True) + r.e_wide[q, STRETCH - 1 :, :] * jnp.sum(
+        at_last = r.at_last[q] + r.e_wide[q, STRETCH - 1 :, :] * jnp.sum(
             r.s_all[q] * r.d_all[q], axis=0, keepdims=True
         )
         at_last = times_exact(jnp.broadcast_to(at_last, (8, width)), gather)[:1]
         d_sum = exact_times(upper, d_cum) + at_last
         r.gd_wide[q] = (v / dt + rate * d_sum) * jax.nn.sigmoid(r.raw[q])
+        r.y_out[q] = (y + skip_row * x_of(q).astype(F32)).astype(BF16)
 
     def send_steps():
         for q in range(seqs):
@@ -470,26 +490,28 @@
         over(nh - 1, one)
         r.gd_all[h] = r.gd_pack[h]
 
-    decays(0)
+    decays(0, 0)
     arrived(r.tot_all.at[0 : ns - 1], TOT)
     r.wide[...] = times_exact(r.tot_all[...].reshape(ns * 8, LANES), spread)
-    scan_back(0)
-    scan_back(1)
+    scan_back(0, 0)
     own[2].wait()
     send_state(0)
-    decays(1)
+    decays(1, 0)
+    scan_back(1, 0)
+    within(0)
     send_state(1)
-    grad_x(0)
-    grad_x(1)
-    within(0)
+    grad_x(0, 0)
     scan_on(0)
     within(1)
+    before_state(0)
+    grad_b(0)
+    grad_x(1, 0)
     scan_on(1)
-    grad_b(0)
     grad_b(1)
+    before_state(1)
     join_b(0)
+    grad_c(0)
     join_b(1)
-    grad_c(0)
     outputs(0)
     join_c(0)
     grad_c(1)
@@ -514,8 +536,9 @@
     left(r.tot_all.at[0 : ns - 1], TOT)
     for q in range(seqs):
         left(r.x_all.at[q, 0 : nh - 1], X + q)
-        left(r.g_in.at[q, 0 : ns - 1], G + q)
-        left(r.g_res.at[q, 0 : ns - 1], D + q)
+        for c in range(CUTS):
+            left(r.g_in.at[q, 0 : ns - 1, :, piece(c)], G + q * CUTS + c)
+            left(r.g_res.at[q, 0 : ns - 1, :, piece(c)], D + q * CUTS + c)
         left(r.f_in.at[q, 0 : ns - 1], F + q)
         left(r.f_res.at[q, 0 : ns - 1], S + q)
         left(r.gx.at[q, 0 : (nh - 1) * rows, :], GX + q)
@@ -574,6 +597,9 @@
         "mix_hi": ((seqs, heads, STRETCH, STRETCH), BF16),
         "mix_lo": ((seqs, heads, STRETCH, STRETCH), BF16),
         "z_t": ((seqs, width, STRETCH), F32),
+        "v": ((seqs, STRETCH, LANES), F32),
+        "at_last": ((seqs, 1, width), F32),
+        "gc_in": ((seqs, STRETCH, STATE), F32),
         "xc": ((seqs, STRETCH, width), F32),
         "xp": ((seqs, STRETCH, width), F32),
         "y_in": ((seqs, STRETCH, width), F32),
@@ -594,7 +620,7 @@
         scratch[name + "_all"] = ((seqs, STATE, width), F32)
         scratch[name + "_code"] = ((seqs, STATE, width), BF16)
         scratch[name + "_bound"] = ((seqs, ns, 1, width), F32)
-    sems = 7 + 10 * seqs
+    sems = 7 + (8 + 2 * CUTS) * seqs
     names = (
         ["a_log", "skip", "x_in", "b_in", "c_in", "dt_in", "gy_in"]
         + ["y_out", "gx_out", "gb_out", "gc_out", "gdt_out"]
@@ -622,7 +648,7 @@
         + [
             pltpu.SemaphoreType.DMA((sems,)),
             pltpu.SemaphoreType.DMA((sems,)),
-            pltpu.SemaphoreType.DMA((4 + 3 * seqs,)),
+            pltpu.SemaphoreType.DMA((4 + (CUTS + 2) * seqs,)),
         ],
         compiler_params=pltpu.CompilerParams(
             collective_id=0, has_side_effects=True, vmem_limit_bytes=56 * 1024 * 1024

time: 57.6 us -> 57.2 us (level)
  no operation moved by 1% of the time
where the time goes in v4:
time: 57.2 us; the launch traced here: 57 us
  Pallas kernels  56.4 us (99%)
  between operations  0.64 us (1%)
    pallas_call x1, Pallas kernels, on_device(): pl.pallas_call(body, out_shape=tuple((pltpu.VMEM(array.shape, BF16) for a...  55.3 us

profile of v4, /device:TPU:1, one launch (start us, length us, event | category | flops | bytes accessed | tf_op | source)
XLA Modules:
  0.0 57.0 jit_solution(5798358189836669050)
XLA Ops:
  0.6 55.3 %mixer.1 = (bf16[2,256,512]{2,1,0:T(8,128)(2,1)S(1)}, bf16[2,16,8192]{2,1,0:T(8,128)(2,1)S(1)}, bf16[2,16,2048]{2,1,0:T(8,128)(2,1)S(1)}, bf16[2,16,2048]{2,1,0:T(8,128)(2,1)S(1)}, bf16[2,16,128]{2,1,0:T(8,128)(2,1)S(1)}) custom-call(f32[8]{0:T(128)} %refs_0_.1, f32[8]{0:T(128)} %refs_1_.1, bf16[2,16,8192]{2,1,0:T(8,128)(2,1)} %refs_2_.1, ...), custom_call_target="tpu_custom_call" | custom-call | tf_op jit(solution)/shard_map/mixer/pallas_call | solution.py:642
  55.9 1.1 %deliver.1 = (bf16[2,256,512]{2,1,0:T(8,128)(2,1)}, bf16[2,16,8192]{2,1,0:T(8,128)(2,1)}, bf16[2,16,2048]{2,1,0:T(8,128)(2,1)}, bf16[2,16,2048]{2,1,0:T(8,128)(2,1)}, bf16[2,16,128]{2,1,0:T(8,128)(2,1)}) custom-call(bf16[2,256,512]{2,1,0:T(8,128)(2,1)S(1)} %get-tuple-element.10.refs_0_, bf16[2,16,8192]{2,1,0:T(8,128)(2,1)S(1)} %get-tuple-element.11.refs_1_, ...), custom_call_target="tpu_custom_call" | custom-call | tf_op jit(solution)/shard_map/deliver/pallas_call | solution.py:659
